TPU v7x, 256 devices: a whole 4x4x8 slice. The times are simulated.
256 devices in a mesh: gx: 8 (over y, core), gy: 32 (over x, z).
Axes of the slice: x: 4, y: 4, z: 8, core: 2. Of those that a mesh axis runs over, the one named last changes fastest.
Arguments:
- values: bfloat16 [8, 8, 32, 2048], P(None, 'gx', 'gy'), may hold values from -6 to 6
- point_slot: int32 [8, 32, 2048], P('gx', 'gy'), may hold values from 0 to 2047, each once within a row
- leaf_basis: bfloat16 [32, 128, 128, 64], P('gx', 'gy'), may hold values from -0.5 to 0.5
- near_blocks: bfloat16 [32, 128, 9, 128, 128], P('gx', 'gy'), may hold values from -0.1875 to 0.1875
- transfer_leaf: bfloat16 [32, 128, 64, 64], P('gx', 'gy'), may hold values from -0.5 to 0.5
- transfer_mid: bfloat16 [16, 64, 64, 64], P('gx', 'gy'), may hold values from -0.5 to 0.5
- transfer_dev: bfloat16 [8, 32, 64, 64], P('gx', 'gy'), may hold values from -0.5 to 0.5
- transfer_coarse: bfloat16 [4, 16, 64, 64], replicated, may hold values from -0.5 to 0.5
- coupling_leaf: bfloat16 [32, 128, 36, 64, 64], P('gx', 'gy'), may hold values from -0.15625 to 0.15625
- coupling_mid: bfloat16 [16, 64, 36, 64, 64], P('gx', 'gy'), may hold values from -0.15625 to 0.15625
- coupling_dev: bfloat16 [8, 32, 36, 64, 64], P('gx', 'gy'), may hold values from -0.15625 to 0.15625
- coupling_coarse: bfloat16 [8, 32, 36, 16, 64], P('gx', 'gy'), may hold values from -0.15625 to 0.15625
- coupling_top: bfloat16 [8, 32, 16, 4, 64], P('gx', 'gy'), may hold values from -0.21875 to 0.21875
Outputs:
- first_product: float32 [8, 8, 32, 2048], P(None, 'gx', 'gy')
- second_product: float32 [8, 8, 32, 2048], P(None, 'gx', 'gy')
Inputs may be any that keep to these rules, and one draw needn't show every extreme that they name: `point_slot`: every device's entries along the last dimension are a permutation of 0 to 2047.
All inputs are finite; a program needn't handle non-finite values.
Results may differ from a plain program's by a relative error of at most 0.025.
Values may be sent and summed in bfloat16 or wider, within the bound.
A program may use at most 128 MiB of HBM per device.

v0:
```python
import jax
import jax.numpy as jnp
import numpy as np
from jax import lax
from jax.sharding import PartitionSpec as P


def with_halo(cells, sides, width):
    for axis, dim in sides:
        count = lax.axis_size(axis)
        ends = count - 1
        head = lax.slice_in_dim(cells, 0, width, axis=dim)
        tail = lax.slice_in_dim(cells, cells.shape[dim] - width, cells.shape[dim], axis=dim)
        cells = jnp.concatenate(
            [
                lax.ppermute(tail, axis, [(i, (i + 1) % count) for i in range(ends)]),
                cells,
                lax.ppermute(head, axis, [((i + 1) % count, i) for i in range(ends)]),
            ],
            axis=dim,
        )
    return cells


def slot_table():
    mask_table = np.ones((2, 2, 36), np.float32)
    for row_bit in range(2):
        for col_bit in range(2):
            for slot_index in range(36):
                if (
                    abs(slot_index // 6 - 2 - row_bit) <= 1
                    and abs(slot_index % 6 - 2 - col_bit) <= 1
                ):
                    mask_table[row_bit, col_bit, slot_index] = 0.0
    return mask_table


def lift_local(coeffs, transfer):
    vectors, row_count, col_count, span_width = coeffs.shape
    child_terms = jnp.einsum(
        "rabk,abkm->rabm", coeffs, transfer, preferred_element_type=jnp.float32
    )
    child_terms = child_terms.reshape(vectors, row_count // 2, 2, col_count // 2, 2, span_width)
    return child_terms.sum(axis=(2, 4)).astype(jnp.bfloat16)


def far_local(padded, coupling, boxes_side):
    stacked = []
    for slot_index in range(36):
        row_first = slot_index // 6
        col_first = slot_index % 6
        window_piece = padded[
            :, row_first : row_first + boxes_side : 2, col_first : col_first + boxes_side : 2
        ]
        stacked.append(jnp.repeat(jnp.repeat(window_piece, 2, axis=1), 2, axis=2))
    sources = jnp.stack(stacked, axis=3)
    keep_mask = jnp.asarray(
        np.tile(slot_table(), (boxes_side // 2, boxes_side // 2, 1)), sources.dtype
    )
    sources = sources * keep_mask[None, :, :, :, None]
    return jnp.einsum("rabuk,abumk->rabm", sources, coupling, preferred_element_type=jnp.float32)


def far_single(window, coupling, parity_row, parity_col):
    mask_table = jnp.asarray(slot_table(), window.dtype)
    keep_mask = mask_table[parity_row, parity_col]
    flat_window = window.reshape(window.shape[0], 36, window.shape[3]) * keep_mask[None, :, None]
    return jnp.einsum("ruk,umk->rm", flat_window, coupling, preferred_element_type=jnp.float32)


def top_rows(top_coeffs, coupling, target_row, target_col):
    vectors, row_count, col_count, span_width = top_coeffs.shape
    source_box = jnp.arange(row_count * col_count)
    far_enough = (
        jnp.maximum(
            jnp.abs(source_box // col_count - target_row),
            jnp.abs(source_box % col_count - target_col),
        )
        >= 2
    )
    flat_coeffs = top_coeffs.reshape(vectors, row_count * col_count, span_width)
    flat_coeffs = flat_coeffs * far_enough.astype(flat_coeffs.dtype)[None, :, None]
    return jnp.einsum("rtk,tmk->rm", flat_coeffs, coupling, preferred_element_type=jnp.float32)


def upper_levels(all_three, transfer_coarse, coarse_row, coarse_col):
    vectors, half_rows, half_cols, coeff_count = all_three.shape
    three_terms = jnp.einsum(
        "rpqk,pqkm->rpqm", all_three, transfer_coarse, preferred_element_type=jnp.float32
    )
    all_four = three_terms.reshape(vectors, half_rows // 2, 2, half_cols // 2, 2, coeff_count)
    all_four = all_four.sum(axis=(2, 4)).astype(jnp.bfloat16)
    padded_three = jnp.pad(all_three, ((0, 0), (2, 2), (2, 2), (0, 0)))
    window_three = lax.dynamic_slice(
        padded_three,
        (0, 2 * (coarse_row // 2), 2 * (coarse_col // 2), 0),
        (vectors, 6, 6, coeff_count),
    )
    return (all_four, window_three)


def place_rows(gathered_three, gathered_four, grid_rows, grid_cols, row_pos, col_pos, coeff_count):
    vectors = gathered_three.shape[0]
    coarse_row = row_pos // 2
    coarse_col = col_pos // 2
    gathered_three = gathered_three.reshape(vectors, grid_rows, grid_cols, coeff_count // 4)
    far_three = lax.dynamic_slice(
        gathered_three, (0, 2 * coarse_row, 2 * coarse_col, 0), (vectors, 2, 2, coeff_count // 4)
    ).reshape(vectors, coeff_count)
    gathered_four = gathered_four.reshape(vectors, grid_rows, grid_cols, coeff_count // 16)
    gathered_four = jnp.roll(gathered_four, grid_rows // 2, axis=1)
    block_four = lax.dynamic_slice(
        gathered_four,
        (0, 4 * (row_pos // 4), 4 * (col_pos // 4), 0),
        (vectors, 4, 4, coeff_count // 16),
    )
    far_four = block_four.reshape(vectors, 2, 2, 2, 2, coeff_count // 16)
    far_four = far_four.transpose(0, 1, 3, 2, 4, 5).reshape(vectors, coeff_count)
    return (far_three, far_four)


def product(
    values,
    point_slot,
    leaf_basis,
    near_blocks,
    transfer_leaf,
    transfer_mid,
    transfer_dev,
    transfer_coarse,
    coupling_leaf,
    coupling_mid,
    coupling_dev,
    coupling_coarse,
    coupling_top,
):
    vectors = values.shape[0]
    boxes_side = leaf_basis.shape[0]
    leaf_size = leaf_basis.shape[2]
    coeff_count = leaf_basis.shape[3]
    slots = point_slot[0, 0]
    ordered = values[:, 0, 0, :][:, slots]
    leaf_grid = ordered.reshape(vectors, boxes_side, boxes_side, leaf_size)
    widened = with_halo(leaf_grid, (("gx", 1), ("gy", 2)), 1)
    windows = jnp.stack(
        [
            widened[
                :,
                near_index // 3 : near_index // 3 + boxes_side,
                near_index % 3 : near_index % 3 + boxes_side,
            ]
            for near_index in range(9)
        ],
        axis=3,
    )
    near_part = jnp.einsum(
        "rabkt,abkst->rabs", windows, near_blocks, preferred_element_type=jnp.float32
    )
    level_zero = jnp.einsum(
        "rabs,absk->rabk", leaf_grid, leaf_basis, preferred_element_type=jnp.float32
    ).astype(jnp.bfloat16)
    level_one = lift_local(level_zero, transfer_leaf)
    level_two = lift_local(level_one, transfer_mid)
    parent_terms = jnp.einsum(
        "rabk,abkm->rabm", level_two, transfer_dev, preferred_element_type=jnp.float32
    )[:, 0, 0]
    padded_zero = with_halo(level_zero, (("gx", 1), ("gy", 2)), 2)
    far_zero = far_local(padded_zero, coupling_leaf, boxes_side)
    padded_one = with_halo(level_one, (("gx", 1), ("gy", 2)), 2)
    far_one = far_local(padded_one, coupling_mid, boxes_side // 2)
    row_pos = lax.axis_index("gx")
    col_pos = lax.axis_index("gy")
    grid_rows = lax.axis_size("gx")
    grid_cols = lax.axis_size("gy")
    owner_row = (row_pos + grid_rows // 2) % grid_rows
    coarse_row = row_pos // 2
    coarse_col = col_pos // 2
    own_coarse = lax.dynamic_slice(
        transfer_coarse, (coarse_row, coarse_col, 0, 0), (1, 1, coeff_count, coeff_count)
    )[0, 0]
    own_two = level_two[:, 0, 0]
    gathered_two, gathered_terms = (
        lax.all_gather(own_two.astype(jnp.float32)[:, None], ("gx", "gy"), axis=1, tiled=True),
        lax.all_gather(parent_terms[:, None], ("gx", "gy"), axis=1, tiled=True),
    )
    all_two = gathered_two.astype(jnp.bfloat16).reshape(vectors, grid_rows, grid_cols, coeff_count)
    all_terms = gathered_terms.reshape(vectors, grid_rows // 2, 2, grid_cols // 2, 2, coeff_count)
    all_three = all_terms.sum(axis=(2, 4)).astype(jnp.bfloat16)
    all_four, window_three = upper_levels(all_three, transfer_coarse, coarse_row, coarse_col)
    padded_two = jnp.pad(all_two, ((0, 0), (2, 2), (2, 2), (0, 0)))
    window_two = lax.dynamic_slice(
        padded_two, (0, 2 * (row_pos // 2), 2 * (col_pos // 2), 0), (vectors, 6, 6, coeff_count)
    )
    far_two = far_single(window_two, coupling_dev[0, 0], row_pos % 2, col_pos % 2)
    rows_three = far_single(window_three, coupling_coarse[0, 0], coarse_row % 2, coarse_col % 2)
    rows_four = top_rows(all_four, coupling_top[0, 0], owner_row // 4, col_pos // 4)
    gathered_three, gathered_four = (
        lax.all_gather(rows_three[:, None], ("gx", "gy"), axis=1, tiled=True),
        lax.all_gather(rows_four[:, None], ("gx", "gy"), axis=1, tiled=True),
    )
    far_three, far_four = place_rows(
        gathered_three, gathered_four, grid_rows, grid_cols, row_pos, col_pos, coeff_count
    )
    local_three = far_three + jnp.einsum(
        "km,rm->rk", own_coarse, far_four.astype(jnp.bfloat16), preferred_element_type=jnp.float32
    )
    local_two = far_two + jnp.einsum(
        "km,rm->rk",
        transfer_dev[0, 0],
        local_three.astype(jnp.bfloat16),
        preferred_element_type=jnp.float32,
    )
    local_one = far_one + jnp.einsum(
        "abkm,rm->rabk",
        transfer_mid,
        local_two.astype(jnp.bfloat16),
        preferred_element_type=jnp.float32,
    )
    spread_one = jnp.repeat(jnp.repeat(local_one.astype(jnp.bfloat16), 2, axis=1), 2, axis=2)
    local_zero = far_zero + jnp.einsum(
        "abkm,rabm->rabk", transfer_leaf, spread_one, preferred_element_type=jnp.float32
    )
    far_part = jnp.einsum(
        "absk,rabk->rabs",
        leaf_basis,
        local_zero.astype(jnp.bfloat16),
        preferred_element_type=jnp.float32,
    )
    summed = (near_part + far_part).reshape(vectors, boxes_side * boxes_side * leaf_size)
    placed = jnp.zeros(summed.shape, jnp.float32).at[:, slots].set(summed)
    return placed[:, None, None, :]


def local(
    values,
    point_slot,
    leaf_basis,
    near_blocks,
    transfer_leaf,
    transfer_mid,
    transfer_dev,
    transfer_coarse,
    coupling_leaf,
    coupling_mid,
    coupling_dev,
    coupling_coarse,
    coupling_top,
):
    first_product = product(
        values,
        point_slot,
        leaf_basis,
        near_blocks,
        transfer_leaf,
        transfer_mid,
        transfer_dev,
        transfer_coarse,
        coupling_leaf,
        coupling_mid,
        coupling_dev,
        coupling_coarse,
        coupling_top,
    )
    second_product = product(
        first_product.astype(jnp.bfloat16),
        point_slot,
        leaf_basis,
        near_blocks,
        transfer_leaf,
        transfer_mid,
        transfer_dev,
        transfer_coarse,
        coupling_leaf,
        coupling_mid,
        coupling_dev,
        coupling_coarse,
        coupling_top,
    )
    return (first_product, second_product)


def solution(mesh):
    placed = (
        P(None, "gx", "gy", None),
        P("gx", "gy", None),
        P("gx", "gy", None, None),
        P("gx", "gy", None, None, None),
        P("gx", "gy", None, None),
        P("gx", "gy", None, None),
        P("gx", "gy", None, None),
        P(),
        P("gx", "gy", None, None, None),
        P("gx", "gy", None, None, None),
        P("gx", "gy", None, None, None),
        P("gx", "gy", None, None, None),
        P("gx", "gy", None, None, None),
    )
    return jax.shard_map(
        local,
        mesh=mesh,
        in_specs=placed,
        out_specs=(P(None, "gx", "gy", None), P(None, "gx", "gy", None)),
        check_vma=False,
    )
```

profile of v0, /device:TPU:1, one launch (start us, length us, event | category | flops | bytes accessed | tf_op | source)
XLA Modules:
  0.0 773.1 jit_solution(1197816443538096216)
XLA Ops:
  3.3 6.7 gather_fusion
  12.1 5.1 collective-permute-start.9
  30.7 72.5 %all-gather.8 = bf16[256,64,8]{1,2,0:T(8,128)(2,1)S(1)} all-gather(bf16[1,64,8]{1,2,0:T(8,128)(2,1)S(1)} %bitcast.845), channel_id=2, replica_groups=mesh['gx'=8,'gy'=32] {'gx','gy'}, dimensions={0}, use_global_device_ids=true | all-gather | bytes 263168 | tf_op jit(solution)/shard_map/all_gather | solution.py:183
  106.2 63.1 %all-gather.1 = f32[8,256,1,64]{3,0,2,1:T(8,128)S(1)} all-gather(f32[8,1,1,64]{3,0,2,1:T(8,128)S(1)} %convolution_bitcast_fusion.9), channel_id=3, replica_groups=mesh['gx'=8,'gy'=32] {'gx','gy'}, dimensions={1}, use_global_device_ids=true | all-gather | bytes 526336 | tf_op jit(solution)/shard_map/all_gather | solution.py:184
  173.2 63.8 %all-gather.9 = f32[256,16,8]{1,2,0:T(8,128)S(1)} all-gather(f32[1,16,8]{1,2,0:T(8,128)S(1)} %convolution_bitcast_fusion.8), channel_id=4, replica_groups=mesh['gx'=8,'gy'=32] {'gx','gy'}, dimensions={0}, use_global_device_ids=true | all-gather | bytes 131584 | tf_op jit(solution)/shard_map/all_gather | solution.py:198
  251.7 62.1 %all-gather.10 = bf16[256,4,8]{2,1,0:T(4,128)(2,1)S(1)} all-gather(bf16[1,4,8]{2,1,0:T(4,128)(2,1)S(1)} %convolution_bitcast_fusion.13), channel_id=5, replica_groups=mesh['gx'=8,'gy'=32] {'gx','gy'}, dimensions={0}, use_global_device_ids=true | all-gather | bytes 16448 | tf_op jit(solution)/shard_map/all_gather | solution.py:199
  333.0 4.6 collective-permute-start.2
  339.0 4.2 collective-permute-start.6
  350.7 3.8 convolution_bitcast_fusion.1
  378.3 5.6 convolution_add_fusion.1
  385.3 6.2 scatter_custom_fusion
  392.3 8.8 %gather_fusion.1 = bf16[2048,8]{1,0:T(8,128)(2,1)} fusion(bf16[8,2048]{0,1:T(8,128)(2,1)} %convert_element_type.172, s32[2048]{0:T(1024)S(1)} %copy-done.17), kind=kCustom, calls=%fused_computation.1 | custom fusion | bytes 73728 | tf_op jit(solution)/shard_map/gather | solution.py:142
  405.8 4.1 collective-permute-start.21
  414.2 70.3 %all-gather.5 = f32[8,256,1,64]{3,0,2,1:T(8,128)} all-gather(f32[8,1,1,64]{3,0,2,1:T(8,128)S(1)} %convolution_bitcast_fusion.5), channel_id=7, replica_groups=mesh['gx'=8,'gy'=32] {'gx','gy'}, dimensions={1}, use_global_device_ids=true | all-gather | bytes 526336 | tf_op jit(solution)/shard_map/all_gather | solution.py:184
  492.8 4.7 collective-permute-start.13
  499.5 69.3 %all-gather.11 = bf16[256,64,8]{1,2,0:T(8,128)(2,1)S(1)} all-gather(bf16[1,64,8]{1,2,0:T(8,128)(2,1)S(1)} %bitcast.846), channel_id=6, replica_groups=mesh['gx'=8,'gy'=32] {'gx','gy'}, dimensions={0}, use_global_device_ids=true | all-gather | bytes 263168 | tf_op jit(solution)/shard_map/all_gather | solution.py:183
  574.0 63.3 %all-gather.12 = f32[256,16,8]{1,2,0:T(8,128)S(1)} all-gather(f32[1,16,8]{1,2,0:T(8,128)S(1)} %convolution_bitcast_fusion.4), channel_id=8, replica_groups=mesh['gx'=8,'gy'=32] {'gx','gy'}, dimensions={0}, use_global_device_ids=true | all-gather | bytes 131584 | tf_op jit(solution)/shard_map/all_gather | solution.py:198
  642.7 62.1 %all-gather.13 = bf16[256,4,8]{2,1,0:T(4,128)(2,1)S(1)} all-gather(bf16[1,4,8]{2,1,0:T(4,128)(2,1)S(1)} %convolution_bitcast_fusion.12), channel_id=9, replica_groups=mesh['gx'=8,'gy'=32] {'gx','gy'}, dimensions={0}, use_global_device_ids=true | all-gather | bytes 16448 | tf_op jit(solution)/shard_map/all_gather | solution.py:199
  705.0 4.1 collective-permute-start.17
  720.0 4.6 collective-permute-start.14
  726.0 4.0 collective-permute-start.18
  732.0 3.8 convolution_bitcast_fusion
  758.9 5.6 convolution_add_fusion
  765.9 6.2 scatter_custom_fusion.1
  (528 shorter events, 162.5 us)
Async XLA Ops:
  12.1 308.9 %collective-permute-start.9 = (bf16[8,2,2,64]{3,0,2,1:T(8,128)(2,1)}, bf16[8,2,2,64]{3,0,2,1:T(8,128)(2,1)}, u32[]{:S(2)}, u32[]{:S(2)}) collective-permute-start(bf16[8,2,2,64]{3,0,2,1:T(8,128)(2,1)} %reduce_sum.51), channel_id=1, source_target_pairs={{32,0},{64,32},{96,64},{128,96},{160,128},{192,160},{224,192},{33,... | collective-permute-start | bytes 12296 | tf_op jit(solution)/shard_map/ppermute | solution.py:18
  17.3 306.8 %collective-permute-start.8 = (bf16[8,2,2,64]{3,0,2,1:T(8,128)(2,1)}, bf16[8,2,2,64]{3,0,2,1:T(8,128)(2,1)}, u32[]{:S(2)}, u32[]{:S(2)}) collective-permute-start(bf16[8,2,2,64]{3,0,2,1:T(8,128)(2,1)} %reduce_sum.51), channel_id=1, source_target_pairs={{0,32},{32,64},{64,96},{96,128},{128,160},{160,192},{192,224},{1,3... | collective-permute-start | bytes 12296 | tf_op jit(solution)/shard_map/ppermute | solution.py:16
  20.0 311.0 %collective-permute-start.1 = (bf16[8,1,4,128]{3,0,2,1:T(8,128)(2,1)}, bf16[8,1,4,128]{3,0,2,1:T(8,128)(2,1)}, u32[]{:S(2)}, u32[]{:S(2)}) collective-permute-start(bf16[8,1,4,128]{3,0,2,1:T(8,128)(2,1)} %get-tuple-element.109), channel_id=1, source_target_pairs={{32,0},{64,32},{96,64},{128,96},{160,128},{192,160},{224,192},{33,... | collective-permute-start | bytes 24584 | tf_op jit(solution)/shard_map/ppermute | solution.py:18
  23.0 308.0 %collective-permute-start = (bf16[8,1,4,128]{3,0,2,1:T(8,128)(2,1)}, bf16[8,1,4,128]{3,0,2,1:T(8,128)(2,1)}, u32[]{:S(2)}, u32[]{:S(2)}) collective-permute-start(bf16[8,1,4,128]{3,0,2,1:T(8,128)(2,1)} %get-tuple-element.108), channel_id=1, source_target_pairs={{0,32},{32,64},{64,96},{96,128},{128,160},{160,192},{192,224},{1,3... | collective-permute-start | bytes 24584 | tf_op jit(solution)/shard_map/ppermute | solution.py:16
  26.2 302.8 %collective-permute-start.5 = (bf16[8,2,4,64]{3,0,2,1:T(8,128)(2,1)}, bf16[8,2,4,64]{3,0,2,1:T(8,128)(2,1)}, u32[]{:S(2)}, u32[]{:S(2)}) collective-permute-start(bf16[8,2,4,64]{3,0,2,1:T(8,128)(2,1)} %get-tuple-element.107), channel_id=1, source_target_pairs={{32,0},{64,32},{96,64},{128,96},{160,128},{192,160},{224,192},{33,... | collective-permute-start | bytes 24584 | tf_op jit(solution)/shard_map/ppermute | solution.py:18
  321.0 9.2 %collective-permute-start.4 = (bf16[8,2,4,64]{3,0,2,1:T(8,128)(2,1)}, bf16[8,2,4,64]{3,0,2,1:T(8,128)(2,1)S(1)}, u32[]{:S(2)}, u32[]{:S(2)}) collective-permute-start(bf16[8,2,4,64]{3,0,2,1:T(8,128)(2,1)} %get-tuple-element.106), channel_id=1, source_target_pairs={{0,32},{32,64},{64,96},{96,128},{128,160},{160,192},{192,224},{1,3... | collective-permute-start | bytes 24584 | tf_op jit(solution)/shard_map/ppermute | solution.py:16
  324.9 14.1 %collective-permute-start.10 = (bf16[8,6,2,64]{3,0,2,1:T(8,128)(2,1)S(1)}, bf16[8,6,2,64]{3,0,2,1:T(8,128)(2,1)S(1)}, u32[]{:S(2)}, u32[]{:S(2)}) collective-permute-start(bf16[8,6,2,64]{3,0,2,1:T(8,128)(2,1)S(1)} %pad_maximum_fusion.10), channel_id=1, source_target_pairs={{0,1},{1,2},{2,3},{3,4},{4,5},{5,6},{6,7},{7,8},{8,9},{9,10},{10,1... | collective-permute-start | bytes 36872 | tf_op jit(solution)/shard_map/ppermute | solution.py:16
  328.9 14.3 %collective-permute-start.11 = (bf16[8,6,2,64]{3,0,2,1:T(8,128)(2,1)S(1)}, bf16[8,6,2,64]{3,0,2,1:T(8,128)(2,1)S(1)}, u32[]{:S(2)}, u32[]{:S(2)}) collective-permute-start(bf16[8,6,2,64]{3,0,2,1:T(8,128)(2,1)S(1)} %pad_maximum_fusion.10), channel_id=1, source_target_pairs={{1,0},{2,1},{3,2},{4,3},{5,4},{6,5},{7,6},{8,7},{9,8},{10,9},{11,1... | collective-permute-start | bytes 36872 | tf_op jit(solution)/shard_map/ppermute | solution.py:18
  331.7 16.6 %collective-permute-start.3 = (bf16[8,6,1,128]{3,0,2,1:T(8,128)(2,1)S(1)}, bf16[8,6,1,128]{3,0,2,1:T(8,128)(2,1)S(1)}, u32[]{:S(2)}, u32[]{:S(2)}) collective-permute-start(bf16[8,6,1,128]{3,0,2,1:T(8,128)(2,1)S(1)} %get-tuple-element.100), channel_id=1, source_target_pairs={{1,0},{2,1},{3,2},{4,3},{5,4},{6,5},{7,6},{8,7},{9,8},{10,9},{11,1... | collective-permute-start | bytes 36872 | tf_op jit(solution)/shard_map/ppermute | solution.py:18
  333.0 15.3 %collective-permute-start.2 = (bf16[8,6,1,128]{3,0,2,1:T(8,128)(2,1)S(1)}, bf16[8,6,1,128]{3,0,2,1:T(8,128)(2,1)S(1)}, u32[]{:S(2)}, u32[]{:S(2)}) collective-permute-start(bf16[8,6,1,128]{3,0,2,1:T(8,128)(2,1)S(1)} %get-tuple-element.101), channel_id=1, source_target_pairs={{0,1},{1,2},{2,3},{3,4},{4,5},{5,6},{6,7},{7,8},{8,9},{9,10},{10,1... | collective-permute-start | bytes 36872 | tf_op jit(solution)/shard_map/ppermute | solution.py:16
  337.7 16.8 %collective-permute-start.7 = (bf16[8,8,2,64]{3,0,2,1:T(8,128)(2,1)S(1)}, bf16[8,8,2,64]{3,0,2,1:T(8,128)(2,1)S(1)}, u32[]{:S(2)}, u32[]{:S(2)}) collective-permute-start(bf16[8,8,2,64]{3,0,2,1:T(8,128)(2,1)S(1)} %get-tuple-element.93), channel_id=1, source_target_pairs={{1,0},{2,1},{3,2},{4,3},{5,4},{6,5},{7,6},{8,7},{9,8},{10,9},{11,1... | collective-permute-start | bytes 49160 | tf_op jit(solution)/shard_map/ppermute | solution.py:18
  339.0 15.5 %collective-permute-start.6 = (bf16[8,8,2,64]{3,0,2,1:T(8,128)(2,1)S(1)}, bf16[8,8,2,64]{3,0,2,1:T(8,128)(2,1)S(1)}, u32[]{:S(2)}, u32[]{:S(2)}) collective-permute-start(bf16[8,8,2,64]{3,0,2,1:T(8,128)(2,1)S(1)} %get-tuple-element.92), channel_id=1, source_target_pairs={{0,1},{1,2},{2,3},{3,4},{4,5},{5,6},{6,7},{7,8},{8,9},{9,10},{10,1... | collective-permute-start | bytes 49160 | tf_op jit(solution)/shard_map/ppermute | solution.py:16
  405.8 304.4 %collective-permute-start.21 = (bf16[8,2,2,64]{3,0,2,1:T(8,128)(2,1)}, bf16[8,2,2,64]{3,0,2,1:T(8,128)(2,1)}, u32[]{:S(2)}, u32[]{:S(2)}) collective-permute-start(bf16[8,2,2,64]{3,0,2,1:T(8,128)(2,1)} %reduce_sum.65), channel_id=1, source_target_pairs={{32,0},{64,32},{96,64},{128,96},{160,128},{192,160},{224,192},{33,... | collective-permute-start | bytes 12296 | tf_op jit(solution)/shard_map/ppermute | solution.py:18
  409.9 302.1 %collective-permute-start.20 = (bf16[8,2,2,64]{3,0,2,1:T(8,128)(2,1)}, bf16[8,2,2,64]{3,0,2,1:T(8,128)(2,1)}, u32[]{:S(2)}, u32[]{:S(2)}) collective-permute-start(bf16[8,2,2,64]{3,0,2,1:T(8,128)(2,1)} %reduce_sum.65), channel_id=1, source_target_pairs={{0,32},{32,64},{64,96},{96,128},{128,160},{160,192},{192,224},{1,3... | collective-permute-start | bytes 12296 | tf_op jit(solution)/shard_map/ppermute | solution.py:16
  492.8 225.9 %collective-permute-start.13 = (bf16[8,1,4,128]{3,0,2,1:T(8,128)(2,1)}, bf16[8,1,4,128]{3,0,2,1:T(8,128)(2,1)S(1)}, u32[]{:S(2)}, u32[]{:S(2)}) collective-permute-start(bf16[8,1,4,128]{3,0,2,1:T(8,128)(2,1)} %get-tuple-element.105), channel_id=1, source_target_pairs={{32,0},{64,32},{96,64},{128,96},{160,128},{192,160},{224,192},{33,... | collective-permute-start | bytes 24584 | tf_op jit(solution)/shard_map/ppermute | solution.py:18
  497.6 221.1 %collective-permute-start.12 = (bf16[8,1,4,128]{3,0,2,1:T(8,128)(2,1)}, bf16[8,1,4,128]{3,0,2,1:T(8,128)(2,1)S(1)}, u32[]{:S(2)}, u32[]{:S(2)}) collective-permute-start(bf16[8,1,4,128]{3,0,2,1:T(8,128)(2,1)} %get-tuple-element.104), channel_id=1, source_target_pairs={{0,32},{32,64},{64,96},{96,128},{128,160},{160,192},{192,224},{1,3... | collective-permute-start | bytes 24584 | tf_op jit(solution)/shard_map/ppermute | solution.py:16
  705.0 12.3 %collective-permute-start.17 = (bf16[8,2,4,64]{3,0,2,1:T(8,128)(2,1)}, bf16[8,2,4,64]{3,0,2,1:T(8,128)(2,1)S(1)}, u32[]{:S(2)}, u32[]{:S(2)}) collective-permute-start(bf16[8,2,4,64]{3,0,2,1:T(8,128)(2,1)} %get-tuple-element.103), channel_id=1, source_target_pairs={{32,0},{64,32},{96,64},{128,96},{160,128},{192,160},{224,192},{33,... | collective-permute-start | bytes 24584 | tf_op jit(solution)/shard_map/ppermute | solution.py:18
  710.1 8.5 %collective-permute-start.16 = (bf16[8,2,4,64]{3,0,2,1:T(8,128)(2,1)}, bf16[8,2,4,64]{3,0,2,1:T(8,128)(2,1)S(1)}, u32[]{:S(2)}, u32[]{:S(2)}) collective-permute-start(bf16[8,2,4,64]{3,0,2,1:T(8,128)(2,1)} %get-tuple-element.102), channel_id=1, source_target_pairs={{0,32},{32,64},{64,96},{96,128},{128,160},{160,192},{192,224},{1,3... | collective-permute-start | bytes 24584 | tf_op jit(solution)/shard_map/ppermute | solution.py:16
  712.8 13.2 %collective-permute-start.22 = (bf16[8,6,2,64]{3,0,2,1:T(8,128)(2,1)S(1)}, bf16[8,6,2,64]{3,0,2,1:T(8,128)(2,1)S(1)}, u32[]{:S(2)}, u32[]{:S(2)}) collective-permute-start(bf16[8,6,2,64]{3,0,2,1:T(8,128)(2,1)S(1)} %pad_maximum_fusion.11), channel_id=1, source_target_pairs={{0,1},{1,2},{2,3},{3,4},{4,5},{5,6},{6,7},{7,8},{8,9},{9,10},{10,1... | collective-permute-start | bytes 36872 | tf_op jit(solution)/shard_map/ppermute | solution.py:16
  717.3 12.7 %collective-permute-start.23 = (bf16[8,6,2,64]{3,0,2,1:T(8,128)(2,1)S(1)}, bf16[8,6,2,64]{3,0,2,1:T(8,128)(2,1)S(1)}, u32[]{:S(2)}, u32[]{:S(2)}) collective-permute-start(bf16[8,6,2,64]{3,0,2,1:T(8,128)(2,1)S(1)} %pad_maximum_fusion.11), channel_id=1, source_target_pairs={{1,0},{2,1},{3,2},{4,3},{5,4},{6,5},{7,6},{8,7},{9,8},{10,9},{11,1... | collective-permute-start | bytes 36872 | tf_op jit(solution)/shard_map/ppermute | solution.py:18
  718.7 13.1 %collective-permute-start.15 = (bf16[8,6,1,128]{3,0,2,1:T(8,128)(2,1)S(1)}, bf16[8,6,1,128]{3,0,2,1:T(8,128)(2,1)S(1)}, u32[]{:S(2)}, u32[]{:S(2)}) collective-permute-start(bf16[8,6,1,128]{3,0,2,1:T(8,128)(2,1)S(1)} %get-tuple-element.96), channel_id=1, source_target_pairs={{1,0},{2,1},{3,2},{4,3},{5,4},{6,5},{7,6},{8,7},{9,8},{10,9},{11,1... | collective-permute-start | bytes 36872 | tf_op jit(solution)/shard_map/ppermute | solution.py:18
  720.0 11.8 %collective-permute-start.14 = (bf16[8,6,1,128]{3,0,2,1:T(8,128)(2,1)S(1)}, bf16[8,6,1,128]{3,0,2,1:T(8,128)(2,1)S(1)}, u32[]{:S(2)}, u32[]{:S(2)}) collective-permute-start(bf16[8,6,1,128]{3,0,2,1:T(8,128)(2,1)S(1)} %get-tuple-element.97), channel_id=1, source_target_pairs={{0,1},{1,2},{2,3},{3,4},{4,5},{5,6},{6,7},{7,8},{8,9},{9,10},{10,1... | collective-permute-start | bytes 36872 | tf_op jit(solution)/shard_map/ppermute | solution.py:16
  724.6 11.2 %collective-permute-start.19 = (bf16[8,8,2,64]{3,0,2,1:T(8,128)(2,1)S(1)}, bf16[8,8,2,64]{3,0,2,1:T(8,128)(2,1)S(1)}, u32[]{:S(2)}, u32[]{:S(2)}) collective-permute-start(bf16[8,8,2,64]{3,0,2,1:T(8,128)(2,1)S(1)} %get-tuple-element.86), channel_id=1, source_target_pairs={{1,0},{2,1},{3,2},{4,3},{5,4},{6,5},{7,6},{8,7},{9,8},{10,9},{11,1... | collective-permute-start | bytes 49160 | tf_op jit(solution)/shard_map/ppermute | solution.py:18
  726.0 9.9 %collective-permute-start.18 = (bf16[8,8,2,64]{3,0,2,1:T(8,128)(2,1)S(1)}, bf16[8,8,2,64]{3,0,2,1:T(8,128)(2,1)S(1)}, u32[]{:S(2)}, u32[]{:S(2)}) collective-permute-start(bf16[8,8,2,64]{3,0,2,1:T(8,128)(2,1)S(1)} %get-tuple-element.85), channel_id=1, source_target_pairs={{0,1},{1,2},{2,3},{3,4},{4,5},{5,6},{6,7},{7,8},{8,9},{9,10},{10,1... | collective-permute-start | bytes 49160 | tf_op jit(solution)/shard_map/ppermute | solution.py:16
  (33 other events, 1164.9 us)
where the time goes:
time: 780 us; the launch traced here: 773 us
  blocking collectives  526 us (67%)
  local copies, waits for them, and re-layouts  118 us (15%)
  starting transfers between devices  67.7 us (9%)
  matrix products  41 us (5%)
  other arithmetic  18.3 us (2%)
    all_gather x2, blocking collectives, product(): lax.all_gather(own_two.astype(jnp.float32)[:, None], ('gx', 'gy'), axis=1...  142 us
    all_gather x2, blocking collectives, product(): lax.all_gather(parent_terms[:, None], ('gx', 'gy'), axis=1, tiled=True)  133 us
    all_gather x2, blocking collectives, product(): lax.all_gather(rows_three[:, None], ('gx', 'gy'), axis=1, tiled=True)  127 us
    all_gather x2, blocking collectives, product(): lax.all_gather(rows_four[:, None], ('gx', 'gy'), axis=1, tiled=True)  124 us
    unnamed x223, local copies, waits for them, and re-layouts  54.9 us
    ppermute x12, starting transfers between devices, with_halo(): lax.ppermute(tail, axis, [(i, (i + 1) % count) for i in range(ends)])  36.5 us
    ppermute x12, starting transfers between devices, with_halo(): lax.ppermute(head, axis, [((i + 1) % count, i) for i in range(ends)])  31.2 us
    gather x4, local copies, waits for them, and re-layouts, product(): ordered = values[:, 0, 0, :][:, slots]  16.9 us
  transfers between devices with their start and end apart: 24, of which 0 were waited for; matrix products, arithmetic and copies ran while one was open for 10% of the time, Pallas kernels for 0%

commit v1 on v0

v1 whole, which is shorter than its diff:
```python
import functools

import jax
import jax.numpy as jnp
from jax import lax
from jax.experimental import pallas as pl
from jax.experimental.pallas import tpu as pltpu
from jax.sharding import PartitionSpec as P

F32 = jnp.float32
BF16 = jnp.bfloat16
I32 = jnp.int32
MESH = pl.DeviceIdType.MESH
NN = (((1,), (0,)), ((), ()))
NT = (((1,), (1,)), ((), ()))
VMEM_LIMIT = 56 * 2**20

BLOCK_PEERS = [(a, b) for a in range(4) for b in range(4) if a or b]
TOP_PEERS = [(a, b) for b in (3, 5, 1, 7, 4, 2, 6) for a in (1, 0)] + [(1, 0)]
NEXT_TOP = [(1, 1), (1, -1), (1, 0), (0, 1), (0, -1)]
SIBLINGS = [(1, 0), (0, 1), (1, 1)]
BESIDE = [(a, b) for a in (-1, 0, 1) for b in (-1, 0, 1) if a or b]
LOCAL_ARRAYS = 10


def dot(left, right, dims):
    return lax.dot_general(left, right, dims, preferred_element_type=F32)


def permute(blocks, index_row):
    index = jnp.broadcast_to(index_row, (8, 128))
    lane = index & 127
    source = index >> 7
    result = None
    for block, piece in enumerate(blocks):
        taken = jnp.take_along_axis(piece, lane, axis=1, mode="promise_in_bounds")
        result = taken if result is None else jnp.where(source == block, taken, result)
    return result


def prepare_kernel(values_ref, slot_ref, top_ref, grid_ref, inverse_ref, part_ref, part_wide):
    values = jnp.concatenate([values_ref[r, 0].astype(F32) for r in range(8)], axis=0)
    pieces = [values[:, 128 * s : 128 * s + 128] for s in range(16)]
    for m in range(16):
        grid_ref[m] = permute(pieces, slot_ref[0, 0:1, 128 * m : 128 * m + 128])
    slots = slot_ref[0]
    position = lax.broadcasted_iota(I32, (16, 2048), 1)
    own_block = lax.broadcasted_iota(I32, (16, 2048), 0) == (slots >> 7)
    coded = jnp.concatenate(
        [
            jnp.where(own_block, (position >> 7).astype(F32), 0.0),
            jnp.where(own_block, (position & 127).astype(F32), 0.0),
        ],
        axis=0,
    ).astype(BF16)
    own_lane = lax.broadcasted_iota(I32, (128, 2048), 0) == (slots & 127)
    counted = dot(coded, jnp.where(own_lane, 1.0, 0.0).astype(BF16), NT)
    inverse_ref[...] = (counted[:16] * 128.0 + counted[16:]).astype(I32)
    for t in range(16):
        part_wide[4 * (t // 4) : 4 * (t // 4) + 4, 64 * (t % 4) : 64 * (t % 4) + 64] = top_ref[
            0, 0, t
        ].astype(F32)
    part_ref[...] = part_wide[...].astype(BF16)


def place_kernel(ordered_ref, inverse_ref, first_ref, second_ref):
    for which, placed_ref in enumerate((first_ref, second_ref)):
        pieces = [ordered_ref[which, s] for s in range(16)]
        for m in range(16):
            result = permute(pieces, inverse_ref[m : m + 1])
            for r in range(8):
                placed_ref[r, 0, 0:1, 128 * m : 128 * m + 128] = result[r : r + 1]


def keeps(slot, child):
    return abs(slot // 6 - 2 - child // 2) > 1 or abs(slot % 6 - 2 - child % 2) > 1


def far_children(pairs, weight):
    low = lax.broadcasted_iota(I32, (8, 128), 1) < 64
    zero = jnp.zeros((8, 128), F32)
    total = None
    for u in range(18):
        rows = []
        for child in range(4):
            first, second = keeps(u, child), keeps(u + 18, child)
            if first and second:
                rows.append(pairs[u])
            elif first:
                rows.append(jnp.where(low, pairs[u], zero))
            elif second:
                rows.append(jnp.where(low, zero, pairs[u]))
            else:
                rows.append(zero)
        sources = jnp.concatenate(rows, axis=0).astype(BF16)
        matrices = jnp.concatenate([weight(child, u) for child in range(4)], axis=0)
        term = dot(sources, matrices, NT)
        total = term if total is None else total + term
    owner = lax.broadcasted_iota(I32, (8, 256), 1) >> 6
    result = jnp.zeros((8, 256), F32)
    for child in range(4):
        result = result + jnp.where(owner == child, total[8 * child : 8 * child + 8], 0.0)
    return result


def window_mask(row, col, rows, cols):
    slot = lax.broadcasted_iota(I32, (8, 2304), 1) >> 6
    slot_row = (slot * 43) >> 8
    slot_col = slot - 6 * slot_row
    source_row = slot_row + 2 * (row // 2) - 2
    source_col = slot_col + 2 * (col // 2) - 2
    inside = (source_row >= 0) & (source_row < rows) & (source_col >= 0) & (source_col < cols)
    apart = (jnp.abs(source_row - row) > 1) | (jnp.abs(source_col - col) > 1)
    return jnp.where(inside & apart, 1.0, 0.0)


def strip(step):
    return {-1: (2, 6, 2), 0: (2, 2, 4), 1: (4, 0, 2)}[step]


def main_kernel(
    grid_rows,
    grid_cols,
    grid_ref,
    part_ref,
    basis_any,
    near_any,
    e0_any,
    e1_any,
    e2_any,
    e3_any,
    m0_any,
    m1_any,
    m2_any,
    m3_any,
    out_ref,
    basis,
    near,
    e0,
    e1,
    e2,
    e3,
    m0,
    m1,
    m2,
    m3,
    m0_pairs,
    m1_pairs,
    w2,
    w3,
    w4,
    e3_twice,
    e3_spread,
    mask2,
    mask3,
    mask4,
    halo,
    window,
    threes,
    fours,
    pair_tiles,
    near_sum,
    far_zero,
    far_one,
    local_sem,
    block_send,
    block_recv,
    top_send,
    top_recv,
    three_send,
    three_recv,
    side_send,
    side_recv,
    halo_send,
    halo_recv,
    w3_send,
    w3_recv,
    cross_send,
    cross_recv,
    w4_send,
    w4_recv,
):
    i = lax.axis_index("gx")
    j = lax.axis_index("gy")
    in_row, in_col = i % 4, j % 4
    half_row, half_col = in_row // 2, in_col // 2
    row_start, col_start = 2 - 2 * half_row, 2 - 2 * half_col
    own_top = (i // 4) * 8 + j // 4

    def block_peer(a, b):
        return (4 * (i // 4) + (in_row + a) % 4, 4 * (j // 4) + (in_col + b) % 4)

    def top_peer(a, b):
        return ((i + 4 * a) % grid_rows, (j + 4 * b + grid_cols) % grid_cols)

    def beside(a, b):
        return ((i + a + grid_rows) % grid_rows, (j + b + grid_cols) % grid_cols)

    def remote(source, target, send, recv, peer):
        return pltpu.make_async_remote_copy(
            src_ref=source,
            dst_ref=target,
            send_sem=send,
            recv_sem=recv,
            device_id=peer,
            device_id_type=MESH,
        )

    barrier = pltpu.get_barrier_semaphore()
    for a, b in TOP_PEERS:
        pl.semaphore_signal(barrier, 1, device_id=top_peer(a, b), device_id_type=MESH)
    for a, b in BLOCK_PEERS:
        pl.semaphore_signal(barrier, 1, device_id=block_peer(a, b), device_id_type=MESH)
    for a, b in BESIDE:
        pl.semaphore_signal(barrier, 1, device_id=beside(a, b), device_id_type=MESH)

    e3_own = e3_any.at[pl.ds(2 * (i // 4), 2), pl.ds(2 * (j // 4), 2)]
    staged = [
        (basis_any, basis),
        (e0_any, e0),
        (e1_any, e1),
        (e2_any, e2),
        (m3_any, m3),
        (m2_any, m2),
        (e3_own, e3),
        (m1_any, m1),
        (m0_any, m0),
        (near_any, near),
    ]
    loads = [
        pltpu.make_async_copy(source, target, local_sem.at[n])
        for n, (source, target) in enumerate(staged)
    ]
    for load in loads:
        load.start()

    low = lax.broadcasted_iota(I32, (8, 128), 1) < 64

    def up(product, leaf):
        level_zero = [
            dot(leaf[n].astype(BF16), basis[n // 4, n % 4], NN) for n in range(16)
        ]
        level_one = []
        for p in range(4):
            pa, pb = p // 2, p % 2
            children = jnp.concatenate(
                [level_zero[4 * (2 * pa + c // 2) + 2 * pb + c % 2] for c in range(4)], axis=1
            ).astype(BF16)
            transfer = e0[2 * pa : 2 * pa + 2, 2 * pb : 2 * pb + 2].reshape(256, 64)
            level_one.append(dot(children, transfer, NN))
        children = jnp.concatenate(level_one, axis=1).astype(BF16)
        level_two = dot(children, e1[...].reshape(256, 64), NN)
        term = dot(level_two.astype(BF16), e2[0, 0], NN)
        window[product, row_start + in_row, col_start + in_col] = jnp.concatenate(
            [term, level_two], axis=1
        )
        for n in range(16):
            a, b = n // 4, n % 4
            coeffs = jnp.concatenate(
                [level_zero[n], level_one[2 * (a % 2) + b % 2]], axis=1
            )
            halo[product, 2 + a, 2 + b] = jnp.concatenate([leaf[n], coeffs], axis=0).astype(BF16)

    for n in range(4):
        loads[n].wait()
    up(0, [grid_ref[n] for n in range(16)])

    own_three = 2 * (i % 2) + j % 2
    own_four = 8 * half_row + 4 * half_col + own_three
    loads[4].wait()
    for u in range(18):
        w3[own_three, :, 128 * u : 128 * u + 128] = jnp.concatenate(
            [m3[0, 0, 2 * u], m3[0, 0, 2 * u + 1]], axis=1
        )
    loads[5].wait()
    for u in range(18):
        w2[:, 128 * u : 128 * u + 128] = jnp.concatenate(
            [m2[0, 0, 2 * u], m2[0, 0, 2 * u + 1]], axis=1
        )
    loads[6].wait()
    coarse = e3[...].reshape(256, 64)
    e3_twice[...] = jnp.concatenate([coarse, coarse], axis=1)
    spread_row = lax.broadcasted_iota(I32, (256, 64), 0)
    spread_col = lax.broadcasted_iota(I32, (256, 64), 1)
    chosen = spread_col == (spread_row >> 4) * 4 + (spread_row & 3)
    e3_spread[...] = dot(
        jnp.where(chosen, 1.0, 0.0).astype(BF16), e3[half_row, half_col], NT
    ).astype(BF16)
    mask2[...] = window_mask(i, j, grid_rows, grid_cols)
    mask3[...] = window_mask(i // 2, j // 2, grid_rows // 2, grid_cols // 2)
    quarter = lax.broadcasted_iota(I32, (32, 256), 0) >> 3
    top_box = 4 * quarter + (lax.broadcasted_iota(I32, (32, 256), 1) >> 6)
    apart = (jnp.abs((top_box >> 3) - i // 4) > 1) | (jnp.abs((top_box & 7) - j // 4) > 1)
    mask4[...] = jnp.where(apart, 1.0, 0.0)

    def w3_copies():
        return [
            remote(
                w3.at[own_three],
                w3.at[own_three],
                w3_send.at[n],
                w3_recv.at[n],
                (2 * (i // 2) + (i + a) % 2, 2 * (j // 2) + (j + b) % 2),
            )
            for n, (a, b) in enumerate(SIBLINGS)
        ]

    def cross_copy():
        return remote(
            part_ref, w4.at[own_four], cross_send.at[0], cross_recv.at[0], top_peer(1, 0)
        )

    def w4_copies():
        return [
            remote(
                w4.at[own_four], w4.at[own_four], w4_send.at[n], w4_recv.at[n], block_peer(a, b)
            )
            for n, (a, b) in enumerate(BLOCK_PEERS)
        ]

    def top_copies(product):
        return [
            remote(
                fours.at[product, own_top],
                fours.at[product, own_top],
                top_send.at[product, n],
                top_recv.at[product, n],
                top_peer(a, b),
            )
            for n, (a, b) in enumerate(TOP_PEERS)
        ]

    pl.semaphore_wait(barrier, len(TOP_PEERS) + len(BLOCK_PEERS) + len(BESIDE))

    def apply(product, carry):
        block_copies = []
        for n, (a, b) in enumerate(BLOCK_PEERS):
            peer_row, peer_col = block_peer(a, b)
            target_row = in_row + 2 - 2 * ((peer_row % 4) // 2)
            target_col = in_col + 2 - 2 * ((peer_col % 4) // 2)
            block_copies.append(
                remote(
                    window.at[product, row_start + in_row, col_start + in_col],
                    window.at[product, target_row, target_col],
                    block_send.at[product, n],
                    block_recv.at[product, n],
                    (peer_row, peer_col),
                )
            )
        halo_copies = []
        for n, (a, b) in enumerate(BESIDE):
            row_from, row_to, row_count = strip(a)
            col_from, col_to, col_count = strip(b)
            halo_copies.append(
                remote(
                    halo.at[product, pl.ds(row_from, row_count), pl.ds(col_from, col_count)],
                    halo.at[product, pl.ds(row_to, row_count), pl.ds(col_to, col_count)],
                    halo_send.at[product, n],
                    halo_recv.at[product, n],
                    beside(a, b),
                )
            )
        for copy in block_copies:
            copy.start()
        for copy in halo_copies:
            copy.start()

        @pl.when(product == 0)
        def _():
            cross_copy().start()
            for copy in w3_copies():
                copy.start()
            loads[7].wait()
            for n in range(4):
                for u in range(18):
                    m1_pairs[n, u] = jnp.concatenate(
                        [m1[n // 2, n % 2, u], m1[n // 2, n % 2, u + 18]], axis=1
                    )
            loads[8].wait()

            def pack(n, inner):
                for u in range(18):
                    m0_pairs[n, u] = jnp.concatenate(
                        [m0[n // 4, n % 4, u], m0[n // 4, n % 4, u + 18]], axis=1
                    )
                return inner

            lax.fori_loop(0, 16, pack, 0)
            loads[9].wait()

        for copy in block_copies:
            copy.wait_recv()
        rows = []
        for a in range(2):
            sums = []
            for b in range(2):
                total = None
                for c in range(4):
                    tile = window[
                        product,
                        row_start + 2 * a + c // 2,
                        col_start + 2 * b + c % 2,
                    ]
                    total = tile if total is None else total + tile
                sums.append(total)
            rows.append(jnp.where(low, sums[0], pltpu.roll(sums[1], 64, 1)))
        threes[product, 0, 1] = jnp.concatenate(rows, axis=0).astype(BF16)
        fours[product, own_top] = dot(
            jnp.concatenate(rows, axis=1).astype(BF16), e3_twice[...], NN
        )
        for copy in top_copies(product):
            copy.start()
        three_copies = [
            remote(
                threes.at[product, 0, 1],
                threes.at[product, a, 1 - b],
                three_send.at[product, n],
                three_recv.at[product, n],
                top_peer(a, b),
            )
            for n, (a, b) in enumerate(NEXT_TOP)
        ]
        for copy in three_copies:
            copy.start()
        row_from, row_to = 4 - 4 * half_row, 4 * half_row
        col_from, col_to = 4 - 4 * half_col, 4 * half_col
        side_col = 1 - 2 * half_col
        side_copies = []
        for n, (a, b) in enumerate(SIBLINGS):
            source_rows = pl.ds(row_from, 2) if a else pl.ds(row_start, 4)
            target_rows = pl.ds(row_to, 2) if a else pl.ds(row_start, 4)
            source_cols = pl.ds(col_from, 2) if b else pl.ds(col_start, 4)
            target_cols = pl.ds(col_to, 2) if b else pl.ds(col_start, 4)
            side_copies.append(
                remote(
                    window.at[product, source_rows, source_cols],
                    window.at[product, target_rows, target_cols],
                    side_send.at[product, n],
                    side_recv.at[product, n],
                    top_peer(a, b * side_col),
                )
            )
        for copy in side_copies:
            copy.start()

        @pl.when(product == 0)
        def _():
            cross_copy().wait_recv()
            for copy in w4_copies():
                copy.start()

        for copy in halo_copies:
            copy.wait_recv()
        blank = jnp.zeros((16, 128), BF16)

        def clear(cells):
            for a, b in cells:
                halo[product, a, b] = blank

        @pl.when(i == 0)
        def _():
            clear([(a, b) for a in (0, 1) for b in range(8)])

        @pl.when(i == grid_rows - 1)
        def _():
            clear([(a, b) for a in (6, 7) for b in range(8)])

        @pl.when(j == 0)
        def _():
            clear([(a, b) for a in range(8) for b in (0, 1)])

        @pl.when(j == grid_cols - 1)
        def _():
            clear([(a, b) for a in range(8) for b in (6, 7)])

        def near_row(a, inner):
            for b in range(4):
                total = None
                for n in range(9):
                    source = halo[product, a + 1 + n // 3, b + 1 + n % 3].astype(F32)
                    term = dot(source[:8].astype(BF16), near[a, b, n], NT)
                    total = term if total is None else total + term
                near_sum[4 * a + b] = total
            return inner

        lax.fori_loop(0, 4, near_row, 0)

        def coeffs(a, b):
            return halo[product, a, b].astype(F32)[8:]

        for b in range(8):
            column = [coeffs(a, b) for a in range(8)]
            for a in range(5):
                pair_tiles[a, b] = jnp.where(low, column[a], pltpu.roll(column[a + 3], 64, 1))

        def far_parent(p, inner):
            pa, pb = p // 2, p % 2
            pairs = [pair_tiles[2 * pa + u // 6, 2 * pb + u % 6] for u in range(18)]
            far_zero[p] = far_children(
                pairs,
                lambda child, u: m0_pairs[
                    4 * (2 * pa + child // 2) + 2 * pb + child % 2, u
                ],
            )
            return inner

        lax.fori_loop(0, 4, far_parent, 0)
        place = (0, 1, 2, 3, 6, 7)
        one_pairs = [
            jnp.where(
                low,
                pltpu.roll(coeffs(place[u // 6], place[u % 6]), 64, 1),
                coeffs(place[u // 6 + 3], place[u % 6]),
            )
            for u in range(18)
        ]
        far_one[...] = far_children(one_pairs, lambda child, u: m1_pairs[child, u])

        for copy in side_copies:
            copy.wait_recv()
        two_sources = []
        for u in range(18):
            first = window[product, u // 3, 2 * (u % 3)]
            second = window[product, u // 3, 2 * (u % 3) + 1]
            two_sources.append(jnp.where(low, pltpu.roll(first, 64, 1), second))
        two_sources = jnp.where(mask2[...] > 0.0, jnp.concatenate(two_sources, axis=1), 0.0)
        far_two = dot(two_sources.astype(BF16), w2[...], NT)

        @pl.when(product == 0)
        def _():
            for copy in w3_copies():
                copy.wait_recv()

        for copy in three_copies:
            copy.wait_recv()
        three_tiles = [
            [threes[product, a, b].astype(F32) for b in range(3)] for a in range(2)
        ]
        three_sources = jnp.concatenate(
            [
                three_tiles[0 if u // 6 == 1 else 1][u % 3][8 * ((u // 3) % 2) :][:8]
                for u in range(18)
            ],
            axis=1,
        )
        three_sources = jnp.where(mask3[...] > 0.0, three_sources, 0.0)
        far_three = dot(three_sources.astype(BF16), w3[...].reshape(64, 2304), NT)

        for copy in block_copies + halo_copies + three_copies + side_copies:
            copy.wait_send()

        @pl.when(product == 0)
        def _():
            for copy in w4_copies():
                copy.wait_recv()

        for copy in top_copies(product):
            copy.wait_recv()
        quarters = []
        for q in range(4):
            tiles = [fours[product, 4 * q + t] for t in range(4)]
            quarters.append(
                jnp.concatenate(
                    [jnp.where(low, tiles[0], tiles[1]), jnp.where(low, tiles[2], tiles[3])],
                    axis=1,
                )
            )
        four_sources = jnp.where(mask4[...] > 0.0, jnp.concatenate(quarters, axis=0), 0.0)
        crossed = dot(four_sources.astype(BF16), w4[...].reshape(256, 256), NT)
        lane_quarter = (lax.broadcasted_iota(I32, (8, 256), 1) >> 2) & 3
        far_four = jnp.zeros((8, 256), F32)
        for q in range(4):
            far_four = far_four + jnp.where(lane_quarter == q, crossed[8 * q : 8 * q + 8], 0.0)

        local_three = far_three + dot(far_four.astype(BF16), e3_spread[...], NN)
        local_two = far_two + dot(local_three.astype(BF16), e2[0, 0], NT)
        local_one = far_one[...] + dot(local_two.astype(BF16), e1[...].reshape(256, 64), NT)
        results = [None] * 16
        for p in range(4):
            pa, pb = p // 2, p % 2
            transfer = e0[2 * pa : 2 * pa + 2, 2 * pb : 2 * pb + 2].reshape(256, 64)
            local_zero = far_zero[p] + dot(
                local_one[:, 64 * p : 64 * p + 64].astype(BF16), transfer, NT
            )
            for c in range(4):
                a, b = 2 * pa + c // 2, 2 * pb + c % 2
                results[4 * a + b] = near_sum[4 * a + b] + dot(
                    local_zero[:, 64 * c : 64 * c + 64].astype(BF16), basis[a, b], NT
                )
        for n in range(16):
            out_ref[product, n] = results[n]

        @pl.when(product == 0)
        def _():
            up(1, results)

        return carry

    lax.fori_loop(0, 2, apply, 0)
    for product in range(2):
        for copy in top_copies(product):
            copy.wait_send()
    cross_copy().wait_send()
    for copy in w3_copies() + w4_copies():
        copy.wait_send()


def local(
    grid_rows,
    grid_cols,
    values,
    point_slot,
    leaf_basis,
    near_blocks,
    transfer_leaf,
    transfer_mid,
    transfer_dev,
    transfer_coarse,
    coupling_leaf,
    coupling_mid,
    coupling_dev,
    coupling_coarse,
    coupling_top,
):
    whole = pl.BlockSpec(memory_space=pltpu.VMEM)
    left = pl.BlockSpec(memory_space=pl.ANY)
    dma = pltpu.SemaphoreType.DMA
    params = pltpu.CompilerParams(vmem_limit_bytes=VMEM_LIMIT)
    ordered, inverse, part = pl.pallas_call(
        prepare_kernel,
        out_shape=(
            jax.ShapeDtypeStruct((16, 8, 128), F32),
            jax.ShapeDtypeStruct((16, 128), I32),
            jax.ShapeDtypeStruct((16, 256), BF16),
        ),
        in_specs=[whole] * 3,
        out_specs=(whole,) * 3,
        scratch_shapes=[pltpu.VMEM((16, 256), F32)],
        compiler_params=params,
    )(values, point_slot, coupling_top)
    products = pl.pallas_call(
        functools.partial(main_kernel, grid_rows, grid_cols),
        out_shape=jax.ShapeDtypeStruct((2, 16, 8, 128), F32),
        in_specs=[whole, whole] + [left] * LOCAL_ARRAYS,
        out_specs=whole,
        scratch_shapes=[
            pltpu.VMEM((4, 4, 128, 64), BF16),
            pltpu.VMEM((4, 4, 9, 128, 128), BF16),
            pltpu.VMEM((4, 4, 64, 64), BF16),
            pltpu.VMEM((2, 2, 64, 64), BF16),
            pltpu.VMEM((1, 1, 64, 64), BF16),
            pltpu.VMEM((2, 2, 64, 64), BF16),
            pltpu.VMEM((4, 4, 36, 64, 64), BF16),
            pltpu.VMEM((2, 2, 36, 64, 64), BF16),
            pltpu.VMEM((1, 1, 36, 64, 64), BF16),
            pltpu.VMEM((1, 1, 36, 16, 64), BF16),
            pltpu.VMEM((16, 18, 64, 128), BF16),
            pltpu.VMEM((4, 18, 64, 128), BF16),
            pltpu.VMEM((64, 2304), BF16),
            pltpu.VMEM((4, 16, 2304), BF16),
            pltpu.VMEM((16, 16, 256), BF16),
            pltpu.VMEM((256, 128), BF16),
            pltpu.VMEM((256, 64), BF16),
            pltpu.VMEM((8, 2304), F32),
            pltpu.VMEM((8, 2304), F32),
            pltpu.VMEM((32, 256), F32),
            pltpu.VMEM((2, 8, 8, 16, 128), BF16),
            pltpu.VMEM((2, 6, 6, 8, 128), F32),
            pltpu.VMEM((2, 2, 3, 16, 128), BF16),
            pltpu.VMEM((2, 16, 8, 128), F32),
            pltpu.VMEM((5, 8, 8, 128), F32),
            pltpu.VMEM((16, 8, 128), F32),
            pltpu.VMEM((4, 8, 256), F32),
            pltpu.VMEM((8, 256), F32),
            dma((LOCAL_ARRAYS,)),
            dma((2, 15)),
            dma((2, 15)),
            dma((2, 15)),
            dma((2, 15)),
            dma((2, 5)),
            dma((2, 5)),
            dma((2, 3)),
            dma((2, 3)),
            dma((2, 8)),
            dma((2, 8)),
            dma((3,)),
            dma((3,)),
            dma((1,)),
            dma((1,)),
            dma((15,)),
            dma((15,)),
        ],
        compiler_params=pltpu.CompilerParams(
            collective_id=0, has_side_effects=True, vmem_limit_bytes=VMEM_LIMIT
        ),
    )(
        ordered,
        part,
        leaf_basis,
        near_blocks,
        transfer_leaf,
        transfer_mid,
        transfer_dev,
        transfer_coarse,
        coupling_leaf,
        coupling_mid,
        coupling_dev,
        coupling_coarse,
    )
    placed = jax.ShapeDtypeStruct(values.shape, F32)
    return pl.pallas_call(
        place_kernel,
        out_shape=(placed, placed),
        in_specs=[whole] * 2,
        out_specs=(whole,) * 2,
        compiler_params=params,
    )(products, inverse)


def solution(mesh):
    placed = (
        P(None, "gx", "gy", None),
        P("gx", "gy", None),
        P("gx", "gy", None, None),
        P("gx", "gy", None, None, None),
        P("gx", "gy", None, None),
        P("gx", "gy", None, None),
        P("gx", "gy", None, None),
        P(),
        P("gx", "gy", None, None, None),
        P("gx", "gy", None, None, None),
        P("gx", "gy", None, None, None),
        P("gx", "gy", None, None, None),
        P("gx", "gy", None, None, None),
    )
    return jax.shard_map(
        functools.partial(local, mesh.shape["gx"], mesh.shape["gy"]),
        mesh=mesh,
        in_specs=placed,
        out_specs=(P(None, "gx", "gy", None), P(None, "gx", "gy", None)),
        check_vma=False,
    )
```

time: 780 us -> 58.2 us (0.07)
  blocking collectives: 526 us -> 0 us
  local copies, waits for them, and re-layouts: 118 us -> 3.38 us
  starting transfers between devices: 67.7 us -> 0 us
  Pallas kernels: 0 us -> 53.6 us
  matrix products: 41 us -> 0 us
  other arithmetic: 18.3 us -> 0 us
    all_gather x8 -> x0, blocking collectives: 526 us -> none  [the longest x2 142 us: product(): lax.all_gather(own_two.astype(jnp.float32)[:, None], ('gx', 'gy'), axis=1...]
    ppermute x24 -> x0, starting transfers between devices: 67.7 us -> none  [the longest x12 36.5 us: with_halo(): lax.ppermute(tail, axis, [(i, (i + 1) % count) for i in range(ends)])]
    pallas_call x0 -> x3, Pallas kernels: none -> 53.6 us  [the longest x1 49.5 us: local(): pl.pallas_call(functools.partial(main_kernel, grid_rows, grid_cols), out_...]
    unnamed x223 -> x2, local copies, waits for them, and re-layouts: 54.9 us -> 3.38 us
    dot_general x28 -> x0, matrix products: 41 us -> none  [the longest x2 11.2 us: product(): jnp.einsum('absk,rabk->rabs', leaf_basis, local_zero.astype(jnp.bfloat16)...]
    gather x4 -> x0, local copies, waits for them, and re-layouts: 16.9 us -> none  [product(): ordered = values[:, 0, 0, :][:, slots]]
    scatter x2 -> x0, local copies, waits for them, and re-layouts: 12.4 us -> none  [product(): placed = jnp.zeros(summed.shape, jnp.float32).at[:, slots].set(summed)]
    reshape x10 -> x0, local copies, waits for them, and re-layouts: 11.3 us -> none  [the longest x2 3.57 us: place_rows(): gathered_three.reshape(vectors, grid_rows, grid_cols, coeff_count // 4)]
  transfers between devices with their start and end apart: 24 -> 0, of which waited for: 0 -> 0; matrix products, arithmetic and copies ran while one was open for 10% -> 0% of each run, Pallas kernels for 0% -> 0%
where the time goes in v1:
time: 58.2 us; the launch traced here: 57.7 us
  Pallas kernels  53.6 us (92%)
  local copies, waits for them, and re-layouts  3.38 us (6%)
  between operations  0.64 us (1%)
    pallas_call x1, Pallas kernels, local(): pl.pallas_call(functools.partial(main_kernel, grid_rows, grid_cols), out_...  49.5 us
    unnamed x2, local copies, waits for them, and re-layouts  3.38 us
    pallas_call x1, Pallas kernels, local(): pl.pallas_call(place_kernel, out_shape=(placed, placed), in_specs=[whole]...  2.25 us
    pallas_call x1, Pallas kernels, local(): pl.pallas_call(prepare_kernel, out_shape=(jax.ShapeDtypeStruct((16, 8, 12...  1.94 us

profile of v1, /device:TPU:1, one launch (start us, length us, event | category | flops | bytes accessed | tf_op | source)
XLA Modules:
  0.0 57.7 jit_solution(17135954466540043423)
XLA Ops:
  0.6 1.4 %copy.15.values_ref = bf16[8,1,1,2048]{3,2,1,0:T(2,128)(2,1)} copy(bf16[8,1,1,2048]{3,0,2,1:T(8,128)(2,1)} %param.13) | data formatting | bytes 65536 | tf_op args[0]
  2.1 1.9 %shard_map.140 = (f32[16,8,128]{2,1,0:T(8,128)}, s32[16,128]{1,0:T(8,128)}, bf16[16,256]{1,0:T(8,128)(2,1)}) custom-call(bf16[8,1,1,2048]{3,2,1,0:T(2,128)(2,1)} %copy.15.values_ref, s32[1,1,2048]{2,1,0:T(1,128)} %slot_ref.1, bf16[1,1,16,4,64]{4,3,2,1,0:T(4,128)(2,1)} %top_ref.1), custom_call_target="tpu_custom_call" | custom-call | tf_op jit(solution)/shard_map/pallas_call | solution.py:629
  4.0 1.9 %copy.16.basis_any = bf16[4,4,128,64]{3,2,1,0:T(8,128)(2,1)} copy(bf16[4,4,128,64]{2,3,1,0:T(8,128)(2,1)} %param.15) | data formatting | bytes 524288 | tf_op args[2]
  6.0 49.5 %shard_map.141.ordered_ref = f32[2,16,8,128]{3,2,1,0:T(8,128)} custom-call(f32[16,8,128]{2,1,0:T(8,128)} %get-tuple-element.5.grid_ref, bf16[16,256]{1,0:T(8,128)(2,1)} %get-tuple-element.6.part_ref, bf16[4,4,128,64]{3,2,1,0:T(8,128)(2,1)} %copy.16.basis_any, bf16[4,4,9,128,128]{4,3,2,1,0:T(8,128)(2,1)} %near_any.1, bf16[4,4,64,64]{3,2,1,0:T(8,128)(2,1)} %e0_any.1, ...), custom_call_target="tpu_custom_call" | custom-call | tf_op jit(solution)/shard_map/pallas_call | solution.py:641
  55.4 2.3 %shard_map.142 = (f32[8,1,1,2048]{3,2,1,0:T(1,128)}, f32[8,1,1,2048]{3,2,1,0:T(1,128)}) custom-call(f32[2,16,8,128]{3,2,1,0:T(8,128)} %shard_map.141.ordered_ref, s32[16,128]{1,0:T(8,128)} %get-tuple-element.7.inverse_ref), custom_call_target="tpu_custom_call" | custom-call | tf_op jit(solution)/shard_map/pallas_call | solution.py:711

commit v2 on v1

v2 whole, which is shorter than its diff:
```python
import functools

import jax
import jax.numpy as jnp
from jax import lax
from jax.experimental import pallas as pl
from jax.experimental.pallas import tpu as pltpu
from jax.sharding import PartitionSpec as P

F32 = jnp.float32
BF16 = jnp.bfloat16
I32 = jnp.int32
MESH = pl.DeviceIdType.MESH
NN = (((1,), (0,)), ((), ()))
NT = (((1,), (1,)), ((), ()))
VMEM_LIMIT = 56 * 2**20

BLOCK_PEERS = [(a, b) for b in (4, 3, 5, 2, 6, 1, 7) for a in (1, 0)] + [(1, 0)]
TOP_PEERS = [(2, 2), (2, 1), (2, 3), (1, 2), (3, 2), (1, 1), (1, 3), (3, 1), (3, 3)] + [
    (2, 0),
    (0, 2),
    (1, 0),
    (3, 0),
    (0, 1),
    (0, 3),
]
HALF_PEERS = [(a, b) for a in range(2) for b in range(4) if a or b]
BESIDE = [(a, b) for a in (-1, 0, 1) for b in (-1, 0, 1) if a or b]
LOCAL_ARRAYS = 10


def dot(left, right, dims):
    return lax.dot_general(left, right, dims, preferred_element_type=F32)


def permute(blocks, index_row):
    index = jnp.broadcast_to(index_row, (8, 128))
    lane = index & 127
    source = index >> 7
    result = None
    for block, piece in enumerate(blocks):
        taken = jnp.take_along_axis(piece, lane, axis=1, mode="promise_in_bounds")
        result = taken if result is None else jnp.where(source == block, taken, result)
    return result


def place_kernel(ordered_ref, inverse_ref, first_ref, second_ref):
    for which, placed_ref in enumerate((first_ref, second_ref)):
        pieces = [ordered_ref[which, s] for s in range(16)]
        for m in range(16):
            result = permute(pieces, inverse_ref[m : m + 1])
            for r in range(8):
                placed_ref[r, 0, 0:1, 128 * m : 128 * m + 128] = result[r : r + 1]


def keeps(slot, child):
    return abs(slot // 6 - 2 - child // 2) > 1 or abs(slot % 6 - 2 - child % 2) > 1


def far_children(pairs, weight):
    low = lax.broadcasted_iota(I32, (8, 128), 1) < 64
    zero = jnp.zeros((8, 128), F32)
    sources, matrices = [], []
    for u in range(18):
        rows = []
        for child in range(4):
            first, second = keeps(u, child), keeps(u + 18, child)
            if first and second:
                rows.append(pairs[u])
            elif first:
                rows.append(jnp.where(low, pairs[u], zero))
            elif second:
                rows.append(jnp.where(low, zero, pairs[u]))
            else:
                rows.append(zero)
        sources.append(jnp.concatenate(rows, axis=0).astype(BF16))
        matrices.append(jnp.concatenate([weight(child, u) for child in range(4)], axis=0))
    total = dot(jnp.concatenate(sources, axis=1), jnp.concatenate(matrices, axis=1), NT)
    owner = lax.broadcasted_iota(I32, (8, 256), 1) >> 6
    result = jnp.zeros((8, 256), F32)
    for child in range(4):
        result = result + jnp.where(owner == child, total[8 * child : 8 * child + 8], 0.0)
    return result


def window_mask(row, col, rows, cols):
    slot = lax.broadcasted_iota(I32, (8, 2304), 1) >> 6
    slot_row = (slot * 43) >> 8
    slot_col = slot - 6 * slot_row
    source_row = slot_row + 2 * (row // 2) - 2
    source_col = slot_col + 2 * (col // 2) - 2
    inside = (source_row >= 0) & (source_row < rows) & (source_col >= 0) & (source_col < cols)
    apart = (jnp.abs(source_row - row) > 1) | (jnp.abs(source_col - col) > 1)
    return jnp.where(inside & apart, 1.0, 0.0)


def strip(step):
    return {-1: (2, 6, 2), 0: (2, 2, 4), 1: (4, 0, 2)}[step]


def main_kernel(
    grid_rows,
    grid_cols,
    values_ref,
    slot_ref,
    top_ref,
    basis_any,
    near_any,
    e0_any,
    e1_any,
    e2_any,
    e3_any,
    m0_any,
    m1_any,
    m2_any,
    m3_any,
    out_ref,
    inverse_ref,
    basis,
    near,
    e0,
    e1,
    e2,
    e3,
    m0,
    m1,
    m2,
    m3,
    m0_pairs,
    m1_pairs,
    w2,
    w3,
    w4,
    part_wide,
    part,
    e3_twice,
    e3_spread,
    top_matrix,
    rise,
    fall,
    turn,
    lane_hot,
    mask2,
    mask3,
    mask4,
    halo,
    window,
    threes,
    fours,
    pair_tiles,
    near_sum,
    far_zero,
    local_sem,
    block_send,
    block_recv,
    top_send,
    top_recv,
    three_send,
    three_recv,
    side_send,
    side_recv,
    halo_send,
    halo_recv,
    w3_send,
    w3_recv,
    cross_send,
    cross_recv,
    w4_send,
    w4_recv,
):
    i = lax.axis_index("gx")
    j = lax.axis_index("gy")
    pair_row, core = i // 2, i % 2
    patch, depth = j // 8, j % 8
    half = depth // 4
    own_pair = depth // 2

    def block_peer(a, b):
        return (2 * pair_row + (core + a) % 2, 8 * patch + (depth + b) % 8)

    def half_peer(a, b):
        return (2 * pair_row + (core + a) % 2, 8 * patch + 4 * half + (depth + b) % 4)

    def top_peer(a, b):
        return ((i + 2 * a) % grid_rows, (j + 8 * b + grid_cols) % grid_cols)

    def beside(a, b):
        return ((i + a + grid_rows) % grid_rows, (j + b + grid_cols) % grid_cols)

    def remote(source, target, send, recv, peer):
        return pltpu.make_async_remote_copy(
            src_ref=source,
            dst_ref=target,
            send_sem=send,
            recv_sem=recv,
            device_id=peer,
            device_id_type=MESH,
        )

    barrier = pltpu.get_barrier_semaphore()
    for a, b in TOP_PEERS:
        pl.semaphore_signal(barrier, 1, device_id=top_peer(a, b), device_id_type=MESH)
    for a, b in BLOCK_PEERS:
        pl.semaphore_signal(barrier, 1, device_id=block_peer(a, b), device_id_type=MESH)
    for a, b in BESIDE:
        pl.semaphore_signal(barrier, 1, device_id=beside(a, b), device_id_type=MESH)

    e3_own = e3_any.at[pl.ds(pair_row, 1), pl.ds(4 * patch, 4)]
    staged = [
        (basis_any, basis),
        (e0_any, e0),
        (e1_any, e1),
        (e2_any, e2),
        (m3_any, m3),
        (m2_any, m2),
        (e3_own, e3),
        (m1_any, m1),
        (m0_any, m0),
        (near_any, near),
    ]
    loads = [
        pltpu.make_async_copy(source, target, local_sem.at[n])
        for n, (source, target) in enumerate(staged)
    ]
    for load in loads:
        load.start()

    low = lax.broadcasted_iota(I32, (8, 128), 1) < 64

    def coefficients(product, leaf):
        level_zero = [dot(leaf[n].astype(BF16), basis[n // 4, n % 4], NT) for n in range(16)]
        level_one = []
        for p in range(4):
            pa, pb = p // 2, p % 2
            children = jnp.concatenate(
                [level_zero[4 * (2 * pa + c // 2) + 2 * pb + c % 2] for c in range(4)], axis=1
            ).astype(BF16)
            transfer = e0[2 * pa : 2 * pa + 2, 2 * pb : 2 * pb + 2].reshape(256, 64)
            level_one.append(dot(children, transfer, NN))
        for n in range(16):
            a, b = n // 4, n % 4
            coeffs = jnp.concatenate(
                [level_zero[n], level_one[2 * (a % 2) + b % 2]], axis=1
            )
            halo[product, 2 + a, 2 + b] = jnp.concatenate([leaf[n], coeffs], axis=0).astype(BF16)
        return level_one

    slots = slot_ref[0]
    slot_lane = lax.broadcasted_iota(I32, (128, 2048), 0) == (slots & 127)
    lane_hot[...] = jnp.where(slot_lane, 1.0, 0.0).astype(BF16)
    values = values_ref[0, 0].astype(F32)
    stacked = jnp.concatenate([values[:, 128 * s : 128 * s + 128] for s in range(16)], axis=0)
    candidates = dot(stacked.astype(BF16), lane_hot[...], NN)
    slot_block = jnp.broadcast_to(slots >> 7, (8, 2048))
    ordered = jnp.zeros((8, 2048), F32)
    for s in range(16):
        ordered = jnp.where(slot_block == s, candidates[8 * s : 8 * s + 8], ordered)

    for n in range(4):
        loads[n].wait()
    level_one = coefficients(0, [ordered[:, 128 * n : 128 * n + 128] for n in range(16)])
    level_two = dot(
        jnp.concatenate(level_one, axis=1).astype(BF16), e1[...].reshape(256, 64), NN
    )
    term = dot(level_two.astype(BF16), e2[0, 0], NN)
    window[0, 1, core, 2 + depth] = jnp.concatenate(
        [term, level_two], axis=1
    )

    def block_copies(product):
        copies = []
        for n, (a, b) in enumerate(BLOCK_PEERS):
            copies.append(
                remote(
                    window.at[product, 1, core, 2 + depth],
                    window.at[product, 1, core, 2 + depth],
                    block_send.at[product, n],
                    block_recv.at[product, n],
                    block_peer(a, b),
                )
            )
        return copies

    def halo_copies(product):
        copies = []
        for n, (a, b) in enumerate(BESIDE):
            row_from, row_to, row_count = strip(a)
            col_from, col_to, col_count = strip(b)
            copies.append(
                remote(
                    halo.at[product, pl.ds(row_from, row_count), pl.ds(col_from, col_count)],
                    halo.at[product, pl.ds(row_to, row_count), pl.ds(col_to, col_count)],
                    halo_send.at[product, n],
                    halo_recv.at[product, n],
                    beside(a, b),
                )
            )
        return copies

    own_three = 2 * (i % 2) + j % 2
    own_four = 8 * (pair_row % 2) + 4 * (own_pair % 2) + own_three
    other_four = 8 - 8 * (pair_row % 2) + 4 * (own_pair % 2) + own_three
    next_three = 2 * (i % 2) + 1 - j % 2
    three_peers = [
        (2 * (i // 2) + (i + a) % 2, 2 * (j // 2) + (j + b) % 2) for a, b in ((1, 0), (0, 1))
    ]

    def w3_copy(n):
        return remote(
            w3.at[own_three], w3.at[own_three], w3_send.at[n], w3_recv.at[n], three_peers[n]
        )

    def w3_forward():
        return remote(
            w3.at[next_three], w3.at[next_three], w3_send.at[2], w3_recv.at[2], three_peers[0]
        )

    def cross_copies():
        return [
            remote(
                part, w4.at[own_four], cross_send.at[n], cross_recv.at[n], top_peer(a, 0)
            )
            for n, a in enumerate((2, 3 - 2 * (pair_row % 2)))
        ]

    def w4_copies():
        return [
            remote(
                w4.at[which],
                w4.at[which],
                w4_send.at[7 * m + n],
                w4_recv.at[7 * m + n],
                half_peer(a, b),
            )
            for m, which in enumerate((own_four, other_four))
            for n, (a, b) in enumerate(HALF_PEERS)
        ]

    def top_copies(product):
        return [
            remote(
                fours.at[product, pair_row, patch],
                fours.at[product, pair_row, patch],
                top_send.at[product, n],
                top_recv.at[product, n],
                top_peer(a, b),
            )
            for n, (a, b) in enumerate(TOP_PEERS)
        ]

    for t in range(16):
        part_wide[4 * (t // 4) : 4 * (t // 4) + 4, 64 * (t % 4) : 64 * (t % 4) + 64] = top_ref[
            0, 0, t
        ].astype(F32)
    part[...] = part_wide[...].astype(BF16)
    loads[4].wait()
    for u in range(18):
        w3[own_three, :, 128 * u : 128 * u + 128] = jnp.concatenate(
            [m3[0, 0, 2 * u], m3[0, 0, 2 * u + 1]], axis=1
        )
    loads[6].wait()
    coarse = e3[...].reshape(256, 64)
    first_half = lax.broadcasted_iota(I32, (256, 64), 0) < 128
    nothing = jnp.zeros((256, 64), F32)
    coarse = coarse.astype(F32)
    e3_twice[...] = jnp.concatenate(
        [jnp.where(first_half, coarse, nothing), jnp.where(first_half, nothing, coarse)], axis=1
    ).astype(BF16)
    loads[5].wait()

    pl.semaphore_wait(barrier, len(TOP_PEERS) + len(BLOCK_PEERS) + len(BESIDE))
    for copy in block_copies(0):
        copy.start()
    for copy in halo_copies(0):
        copy.start()

    def set_up():
        for copy in cross_copies():
            copy.start()
        loads[7].wait()
        for n in range(4):
            for u in range(18):
                m1_pairs[n, u] = jnp.concatenate(
                    [m1[n // 2, n % 2, u], m1[n // 2, n % 2, u + 18]], axis=1
                )
        loads[8].wait()

        def pack(n, inner):
            for u in range(18):
                m0_pairs[n, u] = jnp.concatenate(
                    [m0[n // 4, n % 4, u], m0[n // 4, n % 4, u + 18]], axis=1
                )
            return inner

        lax.fori_loop(0, 16, pack, 0)
        loads[9].wait()

    def set_up_more():
        for u in range(18):
            w2[:, 128 * u : 128 * u + 128] = jnp.concatenate(
                [m2[0, 0, 2 * u], m2[0, 0, 2 * u + 1]], axis=1
            )
        mask2[...] = window_mask(i, j, grid_rows, grid_cols)
        mask3[...] = window_mask(i // 2, j // 2, grid_rows // 2, grid_cols // 2)
        top_box = lax.broadcasted_iota(I32, (8, 1024), 1) >> 6
        apart = (jnp.abs((top_box >> 3) - i // 4) > 1) | (jnp.abs((top_box & 7) - j // 4) > 1)
        mask4[...] = jnp.where(apart, 1.0, 0.0)
        spread_row = lax.broadcasted_iota(I32, (64, 256), 0)
        spread_col = lax.broadcasted_iota(I32, (64, 256), 1)
        chosen = spread_row == (spread_col >> 4) * 4 + (spread_col & 3)
        spread = dot(e3[0, own_pair], jnp.where(chosen, 1.0, 0.0).astype(BF16), NN)
        for q in range(4):
            e3_spread[q] = jnp.where(((spread_col >> 2) & 3) == q, spread, 0.0).astype(BF16)
        total = None
        for n in range(16):
            a, b = n // 4, n % 4
            two = dot(e0[a, b], e1[a // 2, b // 2], NN)
            both = jnp.concatenate([dot(two.astype(BF16), e2[0, 0], NN), two], axis=1)
            up = dot(basis[a, b].astype(F32).T.astype(BF16), both.astype(BF16), NN)
            rise[n] = up.astype(BF16)
            fall[:, 128 * n : 128 * n + 128] = up.T.astype(BF16)
            around = dot(up.T.astype(BF16), up.astype(BF16), NN)
            total = around if total is None else total + around
        turn[...] = total.astype(BF16)
        slot_hot = lax.broadcasted_iota(I32, (16, 2048), 0) == (slot_ref[0] >> 7)
        position = lax.broadcasted_iota(I32, (16, 2048), 1)
        coded = jnp.concatenate(
            [
                jnp.where(slot_hot, (position >> 7).astype(F32), 0.0),
                jnp.where(slot_hot, (position & 127).astype(F32), 0.0),
            ],
            axis=0,
        ).astype(BF16)
        counted = dot(coded, lane_hot[...], NT)
        inverse_ref[...] = (counted[:16] * 128.0 + counted[16:]).astype(I32)

    def apply(product, carry):
        @pl.when(product == 0)
        def _():
            set_up_more()
            set_up()

        def near_part(outside):
            for n in range(16):
                a, b = n // 4, n % 4
                places = [
                    m
                    for m in range(9)
                    if outside
                    != (0 <= a + m // 3 - 1 < 4 and 0 <= b + m % 3 - 1 < 4)
                ]
                if not places:
                    continue
                sources = jnp.concatenate(
                    [
                        halo[product, a + 1 + m // 3, b + 1 + m % 3].astype(F32)[:8]
                        for m in places
                    ],
                    axis=1,
                ).astype(BF16)
                blocks = jnp.concatenate([near[a, b, m] for m in places], axis=1)
                total = dot(sources, blocks, NT)
                near_sum[n] = near_sum[n] + total if outside else total

        near_part(False)

        for copy in block_copies(product):
            copy.wait_recv()
        sums = []
        for b in range(4):
            tiles = [window[product, 1, c // 2, 2 + 2 * b + c % 2] for c in range(4)]
            sums.append((tiles[0] + tiles[1]) + (tiles[2] + tiles[3]))
        rows = [
            jnp.where(low, sums[2 * h], pltpu.roll(sums[2 * h + 1], 64, 1)) for h in range(2)
        ]
        fours[product, pair_row, patch] = dot(
            jnp.concatenate(rows, axis=1).astype(BF16), e3_twice[...], NN
        )
        for copy in top_copies(product):
            copy.start()
        for h in range(2):
            threes[product, pair_row, 0, h] = rows[h]
        step = 1 - 2 * half
        three_copies = []
        for a in range(1, 4):
            three_copies.append((threes.at[product, pair_row, 0], threes.at[product, pair_row, 0], a, 0))
        for a in range(4):
            three_copies.append(
                (
                    threes.at[product, pair_row, 0, 1 - half],
                    threes.at[product, pair_row, 1, 1 - half],
                    a,
                    step,
                )
            )
        three_copies = [
            remote(
                source,
                target,
                three_send.at[product, n],
                three_recv.at[product, n],
                top_peer(a, b),
            )
            for n, (source, target, a, b) in enumerate(three_copies)
        ]
        for copy in three_copies:
            copy.start()
        inner_cols = pl.ds(2 + 2 * half, 6)
        side_from, side_to = pl.ds(8 - 6 * half, 2), pl.ds(10 * half, 2)
        side_copies = [
            remote(
                window.at[product, 1, :, source_cols],
                window.at[product, row, :, target_cols],
                side_send.at[product, n],
                side_recv.at[product, n],
                top_peer(a, b),
            )
            for n, (row, source_cols, target_cols, a, b) in enumerate(
                (
                    (0, inner_cols, inner_cols, 1, 0),
                    (2, inner_cols, inner_cols, 3, 0),
                    (0, side_from, side_to, 1, step),
                    (1, side_from, side_to, 0, step),
                    (2, side_from, side_to, 3, step),
                )
            )
        ]
        for copy in side_copies:
            copy.start()

        @pl.when(product == 0)
        def _():
            for copy in cross_copies():
                copy.wait_recv()
            for copy in w4_copies():
                copy.start()
            w3_copy(0).start()
            w3_copy(1).start()

        for copy in halo_copies(product):
            copy.wait_recv()
        blank = jnp.zeros((16, 128), BF16)

        def clear(cells):
            for a, b in cells:
                halo[product, a, b] = blank

        @pl.when(i == 0)
        def _():
            clear([(a, b) for a in (0, 1) for b in range(8)])

        @pl.when(i == grid_rows - 1)
        def _():
            clear([(a, b) for a in (6, 7) for b in range(8)])

        @pl.when(j == 0)
        def _():
            clear([(a, b) for a in range(8) for b in (0, 1)])

        @pl.when(j == grid_cols - 1)
        def _():
            clear([(a, b) for a in range(8) for b in (6, 7)])

        near_part(True)

        @pl.when(product == 0)
        def _():
            w3_copy(1).wait_recv()
            w3_forward().start()

        def coeffs(a, b):
            return halo[product, a, b].astype(F32)[8:]

        for b in range(8):
            column = [coeffs(a, b) for a in range(8)]
            for a in range(5):
                pair_tiles[a, b] = jnp.where(low, column[a], pltpu.roll(column[a + 3], 64, 1))

        def far_parent(p, inner):
            pa, pb = p // 2, p % 2
            pairs = [pair_tiles[2 * pa + u // 6, 2 * pb + u % 6] for u in range(18)]
            far_zero[p] = far_children(
                pairs,
                lambda child, u: m0_pairs[
                    4 * (2 * pa + child // 2) + 2 * pb + child % 2, u
                ],
            )
            return inner

        lax.fori_loop(0, 4, far_parent, 0)
        place = (0, 1, 2, 3, 6, 7)
        one_pairs = [
            jnp.where(
                low,
                pltpu.roll(coeffs(place[u // 6], place[u % 6]), 64, 1),
                coeffs(place[u // 6 + 3], place[u % 6]),
            )
            for u in range(18)
        ]
        local_one = far_children(one_pairs, lambda child, u: m1_pairs[child, u])
        partly = [None] * 16
        for p in range(4):
            pa, pb = p // 2, p % 2
            transfer = e0[2 * pa : 2 * pa + 2, 2 * pb : 2 * pb + 2].reshape(256, 64)
            local_zero = far_zero[p] + dot(
                local_one[:, 64 * p : 64 * p + 64].astype(BF16), transfer, NT
            )
            for c in range(4):
                a, b = 2 * pa + c // 2, 2 * pb + c % 2
                partly[4 * a + b] = near_sum[4 * a + b] + dot(
                    local_zero[:, 64 * c : 64 * c + 64].astype(BF16), basis[a, b], NN
                )
        risen = None
        for n in range(16):
            near_sum[n] = partly[n]
            term = dot(partly[n].astype(BF16), rise[n], NN)
            risen = term if risen is None else risen + term

        for copy in side_copies:
            copy.wait_recv()
        two_sources = []
        for u in range(18):
            first = window[product, u // 6, (u // 3) % 2, 2 * own_pair + 2 * (u % 3)]
            second = window[product, u // 6, (u // 3) % 2, 2 * own_pair + 2 * (u % 3) + 1]
            two_sources.append(jnp.where(low, pltpu.roll(first, 64, 1), second))
        two_sources = jnp.where(mask2[...] > 0.0, jnp.concatenate(two_sources, axis=1), 0.0)
        far_two = dot(two_sources.astype(BF16), w2[...], NT)

        @pl.when(product == 0)
        def _():
            w3_copy(0).wait_recv()
            w3_forward().wait_recv()

        for copy in three_copies:
            copy.wait_recv()
        three_parts = ((1 - half, 1 - half), (0, half), (half, 1 - half))
        three_sources = jnp.concatenate(
            [
                threes[product, (2 * (i // 4) + 2 + u // 3) % 4, side, part_half]
                for u in range(18)
                for side, part_half in (three_parts[u % 3],)
            ],
            axis=1,
        )
        three_sources = jnp.where(mask3[...] > 0.0, three_sources, 0.0)
        far_three = dot(three_sources.astype(BF16), w3[...].reshape(64, 2304), NT)
        far_both = jnp.concatenate([far_three, far_two], axis=1)

        @pl.when(product == 0)
        def _():
            for copy in w4_copies():
                copy.wait_recv()
            rows_four = w4[...].reshape(256, 256)
            for q in range(4):
                top_matrix[0:64, 256 * q : 256 * q + 256] = dot(
                    e3_spread[q], rows_four, NN
                ).astype(BF16)
                top_matrix[64:128, 256 * q : 256 * q + 256] = jnp.zeros((64, 256), BF16)

        for copy in block_copies(product) + halo_copies(product) + three_copies + side_copies:
            copy.wait_send()
        for copy in top_copies(product):
            copy.wait_recv()
        four_sources = jnp.concatenate(
            [
                fours[product, 2 * (t // 4), t % 4] + fours[product, 2 * (t // 4) + 1, t % 4]
                for t in range(8)
            ],
            axis=1,
        )
        four_sources = jnp.where(mask4[...] > 0.0, four_sources, 0.0)
        falling = (far_both + dot(four_sources.astype(BF16), top_matrix[...], NT)).astype(BF16)

        @pl.when(product == 0)
        def _():
            window[1, 1, core, 2 + depth] = risen + dot(
                falling, turn[...], NN
            )
            for copy in block_copies(1):
                copy.start()

        fallen = dot(falling, fall[...], NN)
        results = [near_sum[n] + fallen[:, 128 * n : 128 * n + 128] for n in range(16)]
        for n in range(16):
            out_ref[product, n] = results[n]

        @pl.when(product == 0)
        def _():
            coefficients(1, results)
            for copy in halo_copies(1):
                copy.start()

        return carry

    lax.fori_loop(0, 2, apply, 0)
    for product in range(2):
        for copy in top_copies(product):
            copy.wait_send()
    for copy in [w3_copy(0), w3_copy(1), w3_forward()] + cross_copies() + w4_copies():
        copy.wait_send()


def local(
    grid_rows,
    grid_cols,
    values,
    point_slot,
    leaf_basis,
    near_blocks,
    transfer_leaf,
    transfer_mid,
    transfer_dev,
    transfer_coarse,
    coupling_leaf,
    coupling_mid,
    coupling_dev,
    coupling_coarse,
    coupling_top,
):
    whole = pl.BlockSpec(memory_space=pltpu.VMEM)
    left = pl.BlockSpec(memory_space=pl.ANY)
    dma = pltpu.SemaphoreType.DMA
    params = pltpu.CompilerParams(vmem_limit_bytes=VMEM_LIMIT)
    products, inverse = pl.pallas_call(
        functools.partial(main_kernel, grid_rows, grid_cols),
        out_shape=(
            jax.ShapeDtypeStruct((2, 16, 8, 128), F32),
            jax.ShapeDtypeStruct((16, 128), I32),
        ),
        in_specs=[whole] * 3 + [left] * LOCAL_ARRAYS,
        out_specs=(whole,) * 2,
        scratch_shapes=[
            pltpu.VMEM((4, 4, 64, 128), BF16),
            pltpu.VMEM((4, 4, 9, 128, 128), BF16),
            pltpu.VMEM((4, 4, 64, 64), BF16),
            pltpu.VMEM((2, 2, 64, 64), BF16),
            pltpu.VMEM((1, 1, 64, 64), BF16),
            pltpu.VMEM((1, 4, 64, 64), BF16),
            pltpu.VMEM((4, 4, 36, 64, 64), BF16),
            pltpu.VMEM((2, 2, 36, 64, 64), BF16),
            pltpu.VMEM((1, 1, 36, 64, 64), BF16),
            pltpu.VMEM((1, 1, 36, 16, 64), BF16),
            pltpu.VMEM((16, 18, 64, 128), BF16),
            pltpu.VMEM((4, 18, 64, 128), BF16),
            pltpu.VMEM((64, 2304), BF16),
            pltpu.VMEM((4, 16, 2304), BF16),
            pltpu.VMEM((16, 16, 256), BF16),
            pltpu.VMEM((16, 256), F32),
            pltpu.VMEM((16, 256), BF16),
            pltpu.VMEM((256, 128), BF16),
            pltpu.VMEM((4, 64, 256), BF16),
            pltpu.VMEM((128, 1024), BF16),
            pltpu.VMEM((16, 128, 128), BF16),
            pltpu.VMEM((128, 2048), BF16),
            pltpu.VMEM((128, 128), BF16),
            pltpu.VMEM((128, 2048), BF16),
            pltpu.VMEM((8, 2304), F32),
            pltpu.VMEM((8, 2304), F32),
            pltpu.VMEM((8, 1024), F32),
            pltpu.VMEM((2, 8, 8, 16, 128), BF16),
            pltpu.VMEM((2, 3, 2, 12, 8, 128), F32),
            pltpu.VMEM((2, 4, 2, 2, 8, 128), F32),
            pltpu.VMEM((2, 4, 4, 8, 128), F32),
            pltpu.VMEM((5, 8, 8, 128), F32),
            pltpu.VMEM((16, 8, 128), F32),
            pltpu.VMEM((4, 8, 256), F32),
            dma((LOCAL_ARRAYS,)),
            dma((2, 15)),
            dma((2, 15)),
            dma((2, 15)),
            dma((2, 15)),
            dma((2, 7)),
            dma((2, 7)),
            dma((2, 5)),
            dma((2, 5)),
            dma((2, 8)),
            dma((2, 8)),
            dma((3,)),
            dma((3,)),
            dma((2,)),
            dma((2,)),
            dma((14,)),
            dma((14,)),
        ],
        compiler_params=pltpu.CompilerParams(
            collective_id=0, has_side_effects=True, vmem_limit_bytes=VMEM_LIMIT
        ),
    )(
        jnp.transpose(values, (1, 2, 0, 3)),
        point_slot,
        coupling_top,
        jnp.swapaxes(leaf_basis, 2, 3),
        near_blocks,
        transfer_leaf,
        transfer_mid,
        transfer_dev,
        transfer_coarse,
        coupling_leaf,
        coupling_mid,
        coupling_dev,
        coupling_coarse,
    )
    placed = jax.ShapeDtypeStruct(values.shape, F32)
    return pl.pallas_call(
        place_kernel,
        out_shape=(placed, placed),
        in_specs=[whole] * 2,
        out_specs=(whole,) * 2,
        compiler_params=params,
    )(products, inverse)


def solution(mesh):
    placed = (
        P(None, "gx", "gy", None),
        P("gx", "gy", None),
        P("gx", "gy", None, None),
        P("gx", "gy", None, None, None),
        P("gx", "gy", None, None),
        P("gx", "gy", None, None),
        P("gx", "gy", None, None),
        P(),
        P("gx", "gy", None, None, None),
        P("gx", "gy", None, None, None),
        P("gx", "gy", None, None, None),
        P("gx", "gy", None, None, None),
        P("gx", "gy", None, None, None),
    )
    return jax.shard_map(
        functools.partial(local, mesh.shape["gx"], mesh.shape["gy"]),
        mesh=mesh,
        in_specs=placed,
        out_specs=(P(None, "gx", "gy", None), P(None, "gx", "gy", None)),
        check_vma=False,
    )
```

time: 58.2 us -> 47.3 us (0.81)
  Pallas kernels: 53.6 us -> 46.5 us
  local copies, waits for them, and re-layouts: 3.38 us -> 0 us
    pallas_call x1, Pallas kernels: 49.5 us -> 44.3 us  [local(): pl.pallas_call(functools.partial(main_kernel, grid_rows, grid_cols), out_...]
    unnamed x2 -> x0, local copies, waits for them, and re-layouts: 3.38 us -> none
    pallas_call x1 -> x0, Pallas kernels: 1.94 us -> none  [local(): pl.pallas_call(prepare_kernel, out_shape=(jax.ShapeDtypeStruct((16, 8, 12...]
where the time goes in v2:
time: 47.3 us; the launch traced here: 47.2 us
  Pallas kernels  46.5 us (98%)
  between operations  0.64 us (1%)
    pallas_call x1, Pallas kernels, local(): pl.pallas_call(functools.partial(main_kernel, grid_rows, grid_cols), out_...  44.3 us
    pallas_call x1, Pallas kernels, local(): pl.pallas_call(place_kernel, out_shape=(placed, placed), in_specs=[whole]...  2.25 us

profile of v2, /device:TPU:1, one launch (start us, length us, event | category | flops | bytes accessed | tf_op | source)
XLA Modules:
  0.0 47.2 jit_solution(9757786650049472201)
XLA Ops:
  0.6 44.3 %shard_map.140 = (f32[2,16,8,128]{3,2,1,0:T(8,128)}, s32[16,128]{1,0:T(8,128)}) custom-call(bf16[1,1,8,2048]{3,2,1,0:T(8,128)(2,1)} %bitcast.3, s32[1,1,2048]{2,1,0:T(1,128)} %slot_ref.1, bf16[1,1,16,4,64]{4,3,2,1,0:T(4,128)(2,1)} %top_ref.1, bf16[4,4,64,128]{3,2,1,0:T(8,128)(2,1)} %bitcast.2, bf16[4,4,9,128,128]{4,3,2,1,0:T(8,128)(2,1)} %near_any.1, ...), custom_call_target="tpu_custom_call" | custom-call | tf_op jit(solution)/shard_map/pallas_call | solution.py:724
  44.9 2.3 %shard_map.141 = (f32[8,1,1,2048]{3,2,1,0:T(1,128)}, f32[8,1,1,2048]{3,2,1,0:T(1,128)}) custom-call(f32[2,16,8,128]{3,2,1,0:T(8,128)} %get-tuple-element.4.ordered_ref, s32[16,128]{1,0:T(8,128)} %get-tuple-element.5.inverse_ref), custom_call_target="tpu_custom_call" | custom-call | tf_op jit(solution)/shard_map/pallas_call | solution.py:804

commit v3 on v2

--- a/solution.py
+++ b/solution.py
@@ -61,16 +61,16 @@
     low = lax.broadcasted_iota(I32, (8, 128), 1) < 64
     zero = jnp.zeros((8, 128), F32)
     sources, matrices = [], []
-    for u in range(18):
+    for u, pair in pairs:
         rows = []
         for child in range(4):
-            first, second = keeps(u, child), keeps(u + 18, child)
+            first, second = keeps(2 * u, child), keeps(2 * u + 1, child)
             if first and second:
-                rows.append(pairs[u])
+                rows.append(pair)
             elif first:
-                rows.append(jnp.where(low, pairs[u], zero))
+                rows.append(jnp.where(low, pair, zero))
             elif second:
-                rows.append(jnp.where(low, zero, pairs[u]))
+                rows.append(jnp.where(low, zero, pair))
             else:
                 rows.append(zero)
         sources.append(jnp.concatenate(rows, axis=0).astype(BF16))
@@ -83,10 +83,16 @@
     return result
 
 
-def window_mask(row, col, rows, cols):
+def window_mask(row, col, rows, cols, by_box):
     slot = lax.broadcasted_iota(I32, (8, 2304), 1) >> 6
-    slot_row = (slot * 43) >> 8
-    slot_col = slot - 6 * slot_row
+    if by_box:
+        box = slot >> 2
+        box_row = (box * 11) >> 5
+        slot_row = 2 * box_row + (slot & 1)
+        slot_col = 2 * (box - 3 * box_row) + ((slot >> 1) & 1)
+    else:
+        slot_row = (slot * 43) >> 8
+        slot_col = slot - 6 * slot_row
     source_row = slot_row + 2 * (row // 2) - 2
     source_col = slot_col + 2 * (col // 2) - 2
     inside = (source_row >= 0) & (source_row < rows) & (source_col >= 0) & (source_col < cols)
@@ -145,6 +151,7 @@
     mask4,
     halo,
     window,
+    twos,
     threes,
     fours,
     pair_tiles,
@@ -263,7 +270,7 @@
         jnp.concatenate(level_one, axis=1).astype(BF16), e1[...].reshape(256, 64), NN
     )
     term = dot(level_two.astype(BF16), e2[0, 0], NN)
-    window[0, 1, core, 2 + depth] = jnp.concatenate(
+    window[0, core, depth] = jnp.concatenate(
         [term, level_two], axis=1
     )
 
@@ -272,8 +279,8 @@
         for n, (a, b) in enumerate(BLOCK_PEERS):
             copies.append(
                 remote(
-                    window.at[product, 1, core, 2 + depth],
-                    window.at[product, 1, core, 2 + depth],
+                    window.at[product, core, depth],
+                    window.at[product, core, depth],
                     block_send.at[product, n],
                     block_recv.at[product, n],
                     block_peer(a, b),
@@ -373,35 +380,37 @@
         copy.start()
     for copy in halo_copies(0):
         copy.start()
+    for copy in cross_copies():
+        copy.start()
+    w3_copy(0).start()
+    w3_copy(1).start()
 
     def set_up():
-        for copy in cross_copies():
-            copy.start()
         loads[7].wait()
         for n in range(4):
             for u in range(18):
                 m1_pairs[n, u] = jnp.concatenate(
-                    [m1[n // 2, n % 2, u], m1[n // 2, n % 2, u + 18]], axis=1
+                    [m1[n // 2, n % 2, 2 * u], m1[n // 2, n % 2, 2 * u + 1]], axis=1
                 )
         loads[8].wait()
 
         def pack(n, inner):
             for u in range(18):
                 m0_pairs[n, u] = jnp.concatenate(
-                    [m0[n // 4, n % 4, u], m0[n // 4, n % 4, u + 18]], axis=1
+                    [m0[n // 4, n % 4, 2 * u], m0[n // 4, n % 4, 2 * u + 1]], axis=1
                 )
             return inner
 
         lax.fori_loop(0, 16, pack, 0)
-        loads[9].wait()
 
     def set_up_more():
         for u in range(18):
+            first = 12 * (u // 6) + u % 6
             w2[:, 128 * u : 128 * u + 128] = jnp.concatenate(
-                [m2[0, 0, 2 * u], m2[0, 0, 2 * u + 1]], axis=1
-            )
-        mask2[...] = window_mask(i, j, grid_rows, grid_cols)
-        mask3[...] = window_mask(i // 2, j // 2, grid_rows // 2, grid_cols // 2)
+                [m2[0, 0, first], m2[0, 0, first + 6]], axis=1
+            )
+        mask2[...] = window_mask(i, j, grid_rows, grid_cols, True)
+        mask3[...] = window_mask(i // 2, j // 2, grid_rows // 2, grid_cols // 2, False)
         top_box = lax.broadcasted_iota(I32, (8, 1024), 1) >> 6
         apart = (jnp.abs((top_box >> 3) - i // 4) > 1) | (jnp.abs((top_box & 7) - j // 4) > 1)
         mask4[...] = jnp.where(apart, 1.0, 0.0)
@@ -434,41 +443,68 @@
         counted = dot(coded, lane_hot[...], NT)
         inverse_ref[...] = (counted[:16] * 128.0 + counted[16:]).astype(I32)
 
+    def near_part(product, outside):
+        for n in range(16):
+            a, b = n // 4, n % 4
+            places = [
+                m
+                for m in range(9)
+                if outside
+                != (0 <= a + m // 3 - 1 < 4 and 0 <= b + m % 3 - 1 < 4)
+            ]
+            if not places:
+                continue
+            sources = jnp.concatenate(
+                [
+                    halo[product, a + 1 + m // 3, b + 1 + m % 3].astype(F32)[:8]
+                    for m in places
+                ],
+                axis=1,
+            ).astype(BF16)
+            blocks = jnp.concatenate([near[a, b, m] for m in places], axis=1)
+            total = dot(sources, blocks, NT)
+            near_sum[n] = near_sum[n] + total if outside else total
+
+    def coeffs(product, a, b):
+        return halo[product, a, b].astype(F32)[8:]
+
+    def pair_part(product, outside):
+        for a in range(8):
+            for b in range(4):
+                if outside != (2 <= a < 6 and 1 <= b < 3):
+                    pair_tiles[a, b] = jnp.where(
+                        low,
+                        coeffs(product, a, 2 * b),
+                        pltpu.roll(coeffs(product, a, 2 * b + 1), 64, 1),
+                    )
+        for p in range(4):
+            pa, pb = p // 2, p % 2
+            pairs = []
+            for u in range(18):
+                a, b = 2 * pa + u // 3, pb + u % 3
+                if outside != (2 <= a < 6 and 1 <= b < 3):
+                    pairs.append((u, pair_tiles[a, b]))
+            total = far_children(
+                pairs,
+                lambda child, u: m0_pairs[4 * (2 * pa + child // 2) + 2 * pb + child % 2, u],
+            )
+            far_zero[p] = far_zero[p] + total if outside else total
+
+    def interior(product):
+        near_part(product, False)
+        pair_part(product, False)
+
     def apply(product, carry):
         @pl.when(product == 0)
         def _():
             set_up_more()
             set_up()
-
-        def near_part(outside):
-            for n in range(16):
-                a, b = n // 4, n % 4
-                places = [
-                    m
-                    for m in range(9)
-                    if outside
-                    != (0 <= a + m // 3 - 1 < 4 and 0 <= b + m % 3 - 1 < 4)
-                ]
-                if not places:
-                    continue
-                sources = jnp.concatenate(
-                    [
-                        halo[product, a + 1 + m // 3, b + 1 + m % 3].astype(F32)[:8]
-                        for m in places
-                    ],
-                    axis=1,
-                ).astype(BF16)
-                blocks = jnp.concatenate([near[a, b, m] for m in places], axis=1)
-                total = dot(sources, blocks, NT)
-                near_sum[n] = near_sum[n] + total if outside else total
-
-        near_part(False)
 
         for copy in block_copies(product):
             copy.wait_recv()
         sums = []
         for b in range(4):
-            tiles = [window[product, 1, c // 2, 2 + 2 * b + c % 2] for c in range(4)]
+            tiles = [window[product, c // 2, 2 * b + c % 2] for c in range(4)]
             sums.append((tiles[0] + tiles[1]) + (tiles[2] + tiles[3]))
         rows = [
             jnp.where(low, sums[2 * h], pltpu.roll(sums[2 * h + 1], 64, 1)) for h in range(2)
@@ -505,20 +541,37 @@
         ]
         for copy in three_copies:
             copy.start()
-        inner_cols = pl.ds(2 + 2 * half, 6)
-        side_from, side_to = pl.ds(8 - 6 * half, 2), pl.ds(10 * half, 2)
+        @pl.when(product == 0)
+        def _():
+            for copy in cross_copies():
+                copy.wait_recv()
+            for copy in w4_copies():
+                copy.start()
+
+        for b in range(4):
+            pieces = [
+                jnp.where(
+                    low,
+                    pltpu.roll(window[product, 0, 2 * b + c], 64, 1),
+                    window[product, 1, 2 * b + c],
+                )
+                for c in range(2)
+            ]
+            twos[product, 1, 1 + b] = jnp.concatenate(pieces, axis=0).astype(BF16)
+        inner = pl.ds(1, 4)
+        side_from, side_to = pl.ds(4 - 3 * half, 1), pl.ds(5 * half, 1)
         side_copies = [
             remote(
-                window.at[product, 1, :, source_cols],
-                window.at[product, row, :, target_cols],
+                twos.at[product, 1, source],
+                twos.at[product, row, target],
                 side_send.at[product, n],
                 side_recv.at[product, n],
                 top_peer(a, b),
             )
-            for n, (row, source_cols, target_cols, a, b) in enumerate(
+            for n, (row, source, target, a, b) in enumerate(
                 (
-                    (0, inner_cols, inner_cols, 1, 0),
-                    (2, inner_cols, inner_cols, 3, 0),
+                    (0, inner, inner, 1, 0),
+                    (2, inner, inner, 3, 0),
                     (0, side_from, side_to, 1, step),
                     (1, side_from, side_to, 0, step),
                     (2, side_from, side_to, 3, step),
@@ -530,12 +583,8 @@
 
         @pl.when(product == 0)
         def _():
-            for copy in cross_copies():
-                copy.wait_recv()
-            for copy in w4_copies():
-                copy.start()
-            w3_copy(0).start()
-            w3_copy(1).start()
+            loads[9].wait()
+            interior(0)
 
         for copy in halo_copies(product):
             copy.wait_recv()
@@ -561,42 +610,27 @@
         def _():
             clear([(a, b) for a in range(8) for b in (6, 7)])
 
-        near_part(True)
+        near_part(product, True)
 
         @pl.when(product == 0)
         def _():
             w3_copy(1).wait_recv()
             w3_forward().start()
 
-        def coeffs(a, b):
-            return halo[product, a, b].astype(F32)[8:]
-
-        for b in range(8):
-            column = [coeffs(a, b) for a in range(8)]
-            for a in range(5):
-                pair_tiles[a, b] = jnp.where(low, column[a], pltpu.roll(column[a + 3], 64, 1))
-
-        def far_parent(p, inner):
-            pa, pb = p // 2, p % 2
-            pairs = [pair_tiles[2 * pa + u // 6, 2 * pb + u % 6] for u in range(18)]
-            far_zero[p] = far_children(
-                pairs,
-                lambda child, u: m0_pairs[
-                    4 * (2 * pa + child // 2) + 2 * pb + child % 2, u
-                ],
-            )
-            return inner
-
-        lax.fori_loop(0, 4, far_parent, 0)
-        place = (0, 1, 2, 3, 6, 7)
-        one_pairs = [
-            jnp.where(
-                low,
-                pltpu.roll(coeffs(place[u // 6], place[u % 6]), 64, 1),
-                coeffs(place[u // 6 + 3], place[u % 6]),
-            )
-            for u in range(18)
-        ]
+        pair_part(product, True)
+        one_pairs = []
+        for u in range(18):
+            a, b = (0, 1, 2, 3, 6, 7)[u // 3], (0, 2, 6)[u % 3]
+            one_pairs.append(
+                (
+                    u,
+                    jnp.where(
+                        low,
+                        pltpu.roll(coeffs(product, a, b), 64, 1),
+                        coeffs(product, a, b + 1),
+                    ),
+                )
+            )
         local_one = far_children(one_pairs, lambda child, u: m1_pairs[child, u])
         partly = [None] * 16
         for p in range(4):
@@ -620,9 +654,9 @@
             copy.wait_recv()
         two_sources = []
         for u in range(18):
-            first = window[product, u // 6, (u // 3) % 2, 2 * own_pair + 2 * (u % 3)]
-            second = window[product, u // 6, (u // 3) % 2, 2 * own_pair + 2 * (u % 3) + 1]
-            two_sources.append(jnp.where(low, pltpu.roll(first, 64, 1), second))
+            if u % 2 == 0:
+                tile = twos[product, u // 6, own_pair + (u // 2) % 3].astype(F32)
+            two_sources.append(tile[8 * (u % 2) :][:8])
         two_sources = jnp.where(mask2[...] > 0.0, jnp.concatenate(two_sources, axis=1), 0.0)
         far_two = dot(two_sources.astype(BF16), w2[...], NT)
 
@@ -673,7 +707,7 @@
 
         @pl.when(product == 0)
         def _():
-            window[1, 1, core, 2 + depth] = risen + dot(
+            window[1, core, depth] = risen + dot(
                 falling, turn[...], NN
             )
             for copy in block_copies(1):
@@ -689,6 +723,7 @@
             coefficients(1, results)
             for copy in halo_copies(1):
                 copy.start()
+            interior(1)
 
         return carry
 
@@ -758,10 +793,11 @@
             pltpu.VMEM((8, 2304), F32),
             pltpu.VMEM((8, 1024), F32),
             pltpu.VMEM((2, 8, 8, 16, 128), BF16),
-            pltpu.VMEM((2, 3, 2, 12, 8, 128), F32),
+            pltpu.VMEM((2, 2, 8, 8, 128), F32),
+            pltpu.VMEM((2, 3, 6, 16, 128), BF16),
             pltpu.VMEM((2, 4, 2, 2, 8, 128), F32),
             pltpu.VMEM((2, 4, 4, 8, 128), F32),
-            pltpu.VMEM((5, 8, 8, 128), F32),
+            pltpu.VMEM((8, 4, 8, 128), F32),
             pltpu.VMEM((16, 8, 128), F32),
             pltpu.VMEM((4, 8, 256), F32),
             dma((LOCAL_ARRAYS,)),

time: 47.3 us -> 41.2 us (0.87)
  Pallas kernels: 46.5 us -> 40.3 us
    pallas_call x1, Pallas kernels: 44.3 us -> 38.1 us  [local(): pl.pallas_call(functools.partial(main_kernel, grid_rows, grid_cols), out_...]
where the time goes in v3:
time: 41.2 us; the launch traced here: 41 us
  Pallas kernels  40.3 us (98%)
  between operations  0.64 us (2%)
    pallas_call x1, Pallas kernels, local(): pl.pallas_call(functools.partial(main_kernel, grid_rows, grid_cols), out_...  38.1 us
    pallas_call x1, Pallas kernels, local(): pl.pallas_call(place_kernel, out_shape=(placed, placed), in_specs=[whole]...  2.25 us

profile of v3, /device:TPU:1, one launch (start us, length us, event | category | flops | bytes accessed | tf_op | source)
XLA Modules:
  0.0 41.0 jit_solution(7263133518751514302)
XLA Ops:
  0.6 38.1 %shard_map.140 = (f32[2,16,8,128]{3,2,1,0:T(8,128)}, s32[16,128]{1,0:T(8,128)}) custom-call(bf16[1,1,8,2048]{3,2,1,0:T(8,128)(2,1)} %bitcast.3, s32[1,1,2048]{2,1,0:T(1,128)} %slot_ref.1, bf16[1,1,16,4,64]{4,3,2,1,0:T(4,128)(2,1)} %top_ref.1, bf16[4,4,64,128]{3,2,1,0:T(8,128)(2,1)} %bitcast.2, bf16[4,4,9,128,128]{4,3,2,1,0:T(8,128)(2,1)} %near_any.1, ...), custom_call_target="tpu_custom_call" | custom-call | tf_op jit(solution)/shard_map/pallas_call | solution.py:759
  38.7 2.3 %shard_map.141 = (f32[8,1,1,2048]{3,2,1,0:T(1,128)}, f32[8,1,1,2048]{3,2,1,0:T(1,128)}) custom-call(f32[2,16,8,128]{3,2,1,0:T(8,128)} %get-tuple-element.4.ordered_ref, s32[16,128]{1,0:T(8,128)} %get-tuple-element.5.inverse_ref), custom_call_target="tpu_custom_call" | custom-call | tf_op jit(solution)/shard_map/pallas_call | solution.py:840

commit v4 on v3

--- a/solution.py
+++ b/solution.py
@@ -44,13 +44,39 @@
     return result
 
 
-def place_kernel(ordered_ref, inverse_ref, first_ref, second_ref):
-    for which, placed_ref in enumerate((first_ref, second_ref)):
-        pieces = [ordered_ref[which, s] for s in range(16)]
+def place_kernel(
+    ordered_any,
+    inverse_any,
+    first_any,
+    second_any,
+    ordered,
+    inverse,
+    placed,
+    load_sem,
+    store_sem,
+):
+    loads = [
+        pltpu.make_async_copy(inverse_any, inverse, load_sem.at[2]),
+        pltpu.make_async_copy(ordered_any.at[0], ordered.at[0], load_sem.at[0]),
+        pltpu.make_async_copy(ordered_any.at[1], ordered.at[1], load_sem.at[1]),
+    ]
+    stores = [
+        pltpu.make_async_copy(placed.at[0], first_any, store_sem.at[0]),
+        pltpu.make_async_copy(placed.at[1], second_any, store_sem.at[1]),
+    ]
+    for load in loads:
+        load.start()
+    loads[0].wait()
+    for which in range(2):
+        loads[1 + which].wait()
+        pieces = [ordered[which, s] for s in range(16)]
         for m in range(16):
-            result = permute(pieces, inverse_ref[m : m + 1])
+            result = permute(pieces, inverse[m : m + 1])
             for r in range(8):
-                placed_ref[r, 0, 0:1, 128 * m : 128 * m + 128] = result[r : r + 1]
+                placed[which, r, 0, 0:1, 128 * m : 128 * m + 128] = result[r : r + 1]
+        stores[which].start()
+    for store in stores:
+        store.wait()
 
 
 def keeps(slot, child):
@@ -142,7 +168,6 @@
     e3_twice,
     e3_spread,
     top_matrix,
-    rise,
     fall,
     turn,
     lane_hot,
@@ -420,17 +445,19 @@
         spread = dot(e3[0, own_pair], jnp.where(chosen, 1.0, 0.0).astype(BF16), NN)
         for q in range(4):
             e3_spread[q] = jnp.where(((spread_col >> 2) & 3) == q, spread, 0.0).astype(BF16)
-        total = None
-        for n in range(16):
-            a, b = n // 4, n % 4
-            two = dot(e0[a, b], e1[a // 2, b // 2], NN)
+        for p in range(4):
+            pa, pb = p // 2, p % 2
+            transfer = e0[2 * pa : 2 * pa + 2, 2 * pb : 2 * pb + 2].reshape(256, 64)
+            two = dot(transfer, e1[pa, pb], NN)
             both = jnp.concatenate([dot(two.astype(BF16), e2[0, 0], NN), two], axis=1)
-            up = dot(basis[a, b].astype(F32).T.astype(BF16), both.astype(BF16), NN)
-            rise[n] = up.astype(BF16)
-            fall[:, 128 * n : 128 * n + 128] = up.T.astype(BF16)
-            around = dot(up.T.astype(BF16), up.astype(BF16), NN)
-            total = around if total is None else total + around
-        turn[...] = total.astype(BF16)
+            for c in range(4):
+                a, b = 2 * pa + c // 2, 2 * pb + c % 2
+                rows = both[64 * c : 64 * c + 64].T.astype(BF16)
+                n = 4 * a + b
+                fall[:, 128 * n : 128 * n + 128] = dot(rows, basis[a, b], NN).astype(BF16)
+        turn[...] = dot(fall[...], fall[...], NT).astype(BF16)
+
+    def invert():
         slot_hot = lax.broadcasted_iota(I32, (16, 2048), 0) == (slot_ref[0] >> 7)
         position = lax.broadcasted_iota(I32, (16, 2048), 1)
         coded = jnp.concatenate(
@@ -644,11 +671,9 @@
                 partly[4 * a + b] = near_sum[4 * a + b] + dot(
                     local_zero[:, 64 * c : 64 * c + 64].astype(BF16), basis[a, b], NN
                 )
-        risen = None
         for n in range(16):
             near_sum[n] = partly[n]
-            term = dot(partly[n].astype(BF16), rise[n], NN)
-            risen = term if risen is None else risen + term
+        risen = dot(jnp.concatenate(partly, axis=1).astype(BF16), fall[...], NT)
 
         for copy in side_copies:
             copy.wait_recv()
@@ -724,6 +749,7 @@
             for copy in halo_copies(1):
                 copy.start()
             interior(1)
+            invert()
 
         return carry
 
@@ -785,7 +811,6 @@
             pltpu.VMEM((256, 128), BF16),
             pltpu.VMEM((4, 64, 256), BF16),
             pltpu.VMEM((128, 1024), BF16),
-            pltpu.VMEM((16, 128, 128), BF16),
             pltpu.VMEM((128, 2048), BF16),
             pltpu.VMEM((128, 128), BF16),
             pltpu.VMEM((128, 2048), BF16),
@@ -840,8 +865,15 @@
     return pl.pallas_call(
         place_kernel,
         out_shape=(placed, placed),
-        in_specs=[whole] * 2,
-        out_specs=(whole,) * 2,
+        in_specs=[left] * 2,
+        out_specs=(left,) * 2,
+        scratch_shapes=[
+            pltpu.VMEM((2, 16, 8, 128), F32),
+            pltpu.VMEM((16, 128), I32),
+            pltpu.VMEM((2, 8, 1, 1, 2048), F32),
+            dma((3,)),
+            dma((2,)),
+        ],
         compiler_params=params,
     )(products, inverse)
 

time: 41.2 us -> 39.4 us (0.956)
  Pallas kernels: 40.3 us -> 38.5 us
    pallas_call x1, Pallas kernels: 38.1 us -> 36.1 us  [local(): pl.pallas_call(functools.partial(main_kernel, grid_rows, grid_cols), out_...]
where the time goes in v4:
time: 39.4 us; the launch traced here: 39.1 us
  Pallas kernels  38.5 us (98%)
  between operations  0.64 us (2%)
    pallas_call x1, Pallas kernels, local(): pl.pallas_call(functools.partial(main_kernel, grid_rows, grid_cols), out_...  36.1 us
    pallas_call x1, Pallas kernels, local(): pl.pallas_call(place_kernel, out_shape=(placed, placed), in_specs=[left]...  2.32 us

profile of v4, /device:TPU:1, one launch (start us, length us, event | category | flops | bytes accessed | tf_op | source)
XLA Modules:
  0.0 39.1 jit_solution(1151740324460836474)
XLA Ops:
  0.6 36.1 %shard_map.140 = (f32[2,16,8,128]{3,2,1,0:T(8,128)}, s32[16,128]{1,0:T(8,128)}) custom-call(bf16[1,1,8,2048]{3,2,1,0:T(8,128)(2,1)} %bitcast.3, s32[1,1,2048]{2,1,0:T(1,128)} %slot_ref.1, bf16[1,1,16,4,64]{4,3,2,1,0:T(4,128)(2,1)} %top_ref.1, bf16[4,4,64,128]{3,2,1,0:T(8,128)(2,1)} %bitcast.2, bf16[4,4,9,128,128]{4,3,2,1,0:T(8,128)(2,1)} %near_any.1, ...), custom_call_target="tpu_custom_call" | custom-call | tf_op jit(solution)/shard_map/pallas_call | solution.py:785
  36.8 2.3 %shard_map.141 = (f32[8,1,1,2048]{3,2,1,0:T(1,128)}, f32[8,1,1,2048]{3,2,1,0:T(1,128)}) custom-call(f32[2,16,8,128]{3,2,1,0:T(8,128)} %get-tuple-element.4.ordered_any, s32[16,128]{1,0:T(8,128)} %get-tuple-element.5.inverse_any), custom_call_target="tpu_custom_call" | custom-call | tf_op jit(solution)/shard_map/pallas_call | solution.py:865

commit v5 on v4

--- a/solution.py
+++ b/solution.py
@@ -230,12 +230,12 @@
         )
 
     barrier = pltpu.get_barrier_semaphore()
+    for a, b in BESIDE:
+        pl.semaphore_signal(barrier, 1, device_id=beside(a, b), device_id_type=MESH)
     for a, b in TOP_PEERS:
         pl.semaphore_signal(barrier, 1, device_id=top_peer(a, b), device_id_type=MESH)
     for a, b in BLOCK_PEERS:
         pl.semaphore_signal(barrier, 1, device_id=block_peer(a, b), device_id_type=MESH)
-    for a, b in BESIDE:
-        pl.semaphore_signal(barrier, 1, device_id=beside(a, b), device_id_type=MESH)
 
     e3_own = e3_any.at[pl.ds(pair_row, 1), pl.ds(4 * patch, 4)]
     staged = [
@@ -380,6 +380,11 @@
             for n, (a, b) in enumerate(TOP_PEERS)
         ]
 
+    pl.semaphore_wait(barrier, len(TOP_PEERS) + len(BLOCK_PEERS) + len(BESIDE))
+    for copy in block_copies(0):
+        copy.start()
+    for copy in halo_copies(0):
+        copy.start()
     for t in range(16):
         part_wide[4 * (t // 4) : 4 * (t // 4) + 4, 64 * (t % 4) : 64 * (t % 4) + 64] = top_ref[
             0, 0, t
@@ -400,11 +405,6 @@
     ).astype(BF16)
     loads[5].wait()
 
-    pl.semaphore_wait(barrier, len(TOP_PEERS) + len(BLOCK_PEERS) + len(BESIDE))
-    for copy in block_copies(0):
-        copy.start()
-    for copy in halo_copies(0):
-        copy.start()
     for copy in cross_copies():
         copy.start()
     w3_copy(0).start()

time: 39.4 us -> 39.5 us (level)
  no operation moved by 1% of the time
where the time goes in v5:
time: 39.5 us; the launch traced here: 39.3 us
  Pallas kernels  38.6 us (98%)
  between operations  0.64 us (2%)
    pallas_call x1, Pallas kernels, local(): pl.pallas_call(functools.partial(main_kernel, grid_rows, grid_cols), out_...  36.3 us
    pallas_call x1, Pallas kernels, local(): pl.pallas_call(place_kernel, out_shape=(placed, placed), in_specs=[left]...  2.32 us

profile of v5, /device:TPU:1, one launch (start us, length us, event | category | flops | bytes accessed | tf_op | source)
XLA Modules:
  0.0 39.3 jit_solution(9844728209623025988)
XLA Ops:
  0.6 36.3 %shard_map.140 = (f32[2,16,8,128]{3,2,1,0:T(8,128)}, s32[16,128]{1,0:T(8,128)}) custom-call(bf16[1,1,8,2048]{3,2,1,0:T(8,128)(2,1)} %bitcast.3, s32[1,1,2048]{2,1,0:T(1,128)} %slot_ref.1, bf16[1,1,16,4,64]{4,3,2,1,0:T(4,128)(2,1)} %top_ref.1, bf16[4,4,64,128]{3,2,1,0:T(8,128)(2,1)} %bitcast.2, bf16[4,4,9,128,128]{4,3,2,1,0:T(8,128)(2,1)} %near_any.1, ...), custom_call_target="tpu_custom_call" | custom-call | tf_op jit(solution)/shard_map/pallas_call | solution.py:785
  36.9 2.3 %shard_map.141 = (f32[8,1,1,2048]{3,2,1,0:T(1,128)}, f32[8,1,1,2048]{3,2,1,0:T(1,128)}) custom-call(f32[2,16,8,128]{3,2,1,0:T(8,128)} %get-tuple-element.4.ordered_any, s32[16,128]{1,0:T(8,128)} %get-tuple-element.5.inverse_any), custom_call_target="tpu_custom_call" | custom-call | tf_op jit(solution)/shard_map/pallas_call | solution.py:865
